TPU v7x, 128 devices: a whole 4x4x4 slice. The times are simulated.
128 devices in a mesh: dp: 16 (over y, x_lo, core), group: 8 (over z, x_hi).
Axes of the slice: x: 4 (x_hi: 2, x_lo: 2; x = x_hi * 2 + x_lo), y: 4, z: 4, core: 2. Of those that a mesh axis runs over, the one named last changes fastest.
Arguments:
- tokens: bfloat16 [65536, 4096], P('dp', 'group'), may hold values from -6 to 6
- router_weight: float32 [4096, 256], P('group'), may hold values from -1 to 1
- gate_weight: bfloat16 [8, 4096, 8192], P('group', None, 'dp'), may hold values from -0.09375 to 0.09375
- up_weight: bfloat16 [8, 4096, 8192], P('group', None, 'dp'), may hold values from -0.09375 to 0.09375
- down_weight: bfloat16 [8, 8192, 4096], P('group', 'dp'), may hold values from -2 to 2
- picks: int32 [8, 512], replicated, may hold values from 0 to 65535, as said below
Outputs:
- mixed: bfloat16 [65536, 4096], P('dp', 'group')
Inputs may be any that keep to these rules, and one draw needn't show every extreme that they name: picks holds token indices of 0 to 65535; a token may stand in several slots.
All inputs are finite; a program needn't handle non-finite values.
Results may differ from a plain program's by a relative error of at most 0.013.
Values may be sent and summed in bfloat16 or wider, within the bound.
A program may use at most 128 MiB of HBM per device.

v0:
```python
import jax
import jax.numpy as jnp
from jax import lax
from jax.sharding import PartitionSpec as P


def shards(tokens, router_weight, gate_weight, up_weight, down_weight, picks):
    tok_rows, feat_slice = tokens.shape
    group_size = lax.axis_size("group")
    flight, capacity = picks.shape
    per_group = flight // group_size
    experts = router_weight.shape[1]
    exp_group = experts // group_size
    partial_value = jnp.dot(
        tokens.astype(jnp.float32), router_weight, preferred_element_type=jnp.float32
    )
    logits = lax.psum(partial_value, "group")
    probs = jax.nn.softmax(logits, axis=-1)
    chosen = probs.reshape(tok_rows, group_size, exp_group)[:, :, :per_group].reshape(
        tok_rows, flight
    )
    local_idx = picks - lax.axis_index("dp") * tok_rows
    is_owned = (local_idx >= 0) & (local_idx < tok_rows)
    safe_idx = jnp.clip(local_idx, 0, tok_rows - 1)
    flat_idx = safe_idx.reshape(-1)
    flat_owned = is_owned.reshape(-1)
    taken = jnp.take(tokens, flat_idx, axis=0)
    selected = jnp.where(flat_owned[:, None], taken, jnp.zeros_like(taken))
    selected = selected.reshape(flight, capacity, feat_slice)
    arrived = lax.all_to_all(selected, "group", split_axis=0, concat_axis=2, tiled=True)
    expert_rows = lax.psum(arrived, "dp").astype(jnp.float32).astype(jnp.bfloat16)
    gate_h = jnp.einsum(
        "ecd,edh->ech", expert_rows, gate_weight, preferred_element_type=jnp.float32
    )
    up_h = jnp.einsum("ecd,edh->ech", expert_rows, up_weight, preferred_element_type=jnp.float32)
    hidden = (jax.nn.silu(gate_h) * up_h).astype(jnp.bfloat16)
    partial_out = jnp.einsum(
        "ech,ehd->ecd", hidden, down_weight, preferred_element_type=jnp.float32
    )
    summed_out = lax.psum(partial_out, "dp").astype(jnp.bfloat16)
    returned = lax.all_to_all(summed_out, "group", split_axis=2, concat_axis=0, tiled=True)
    gate_vals = jnp.where(is_owned, jnp.take_along_axis(chosen.T, safe_idx, axis=1), 0.0)
    weighted = (gate_vals[:, :, None] * returned.astype(jnp.float32)).astype(jnp.bfloat16)
    weighted = weighted.reshape(flight * capacity, feat_slice).astype(jnp.float32)
    weighted = jnp.where(flat_owned[:, None], weighted, 0.0)
    mixed = jnp.zeros((tok_rows, feat_slice), jnp.float32).at[flat_idx].add(weighted)
    return mixed.astype(jnp.bfloat16)


def solution(mesh):
    in_specs = (
        P("dp", "group"),
        P("group", None),
        P("group", None, "dp"),
        P("group", None, "dp"),
        P("group", "dp", None),
        P(),
    )
    out_specs = P("dp", "group")
    return jax.shard_map(shards, mesh=mesh, in_specs=in_specs, out_specs=out_specs, check_vma=False)
```

profile of v0, /device:TPU:1, one launch (start us, length us, event | category | flops | bytes accessed | tf_op | source)
XLA Modules:
  0.0 822.9 jit_solution(5572307217673446521)
XLA Ops:
  6.5 1.0 copy-done
  7.6 5.4 fusion.24
  13.0 0.0 all-reduce.6.cloned.1.call-start
  13.1 0.6 copy-done.3
  13.8 20.2 %gather_fusion = bf16[4096,512]{1,0:T(8,128)(2,1)} fusion(bf16[4096,512]{1,0:T(8,128)(2,1)} %param.6, s32[4096]{0:T(1024)S(1)} %broadcast_clamp_fusion), kind=kCustom, calls=%fused_computation | custom fusion | bytes 8404992 | tf_op jit(solution)/shard_map/jit(_take)/gather | solution.py:27
  34.0 6.5 copy.14
  40.5 160.8 %all-reduce.4.cloned.1.call-done = f32[4096,256]{1,0:T(8,128)} async-done(((f32[4096,256]{1,0:T(8,128)}), f32[4096,256]{1,0:T(8,128)}) %all-reduce.4.cloned.1.call-update) | async-done | bytes 4194320 | tf_op jit(solution)/shard_map/psum | solution.py:17
  201.3 2.8 reduce_max.9
  204.1 3.1 fusion.9
  207.2 0.4 copy-done.2
  207.5 3.7 fusion.8
  211.2 5.6 copy.12
  216.9 1.3 slice.8
  218.2 0.6 copy.17
  218.8 27.6 %gather_fusion.1 = f32[4096]{0:T(1024)S(1)} fusion(f32[8,4096]{0,1:T(8,128)S(1)} %bitcast.63, s32[4096]{0:T(1024)S(1)} %bitcast.62), kind=kCustom, calls=%fused_computation.1 | custom fusion | bytes 65536 | tf_op jit(solution)/shard_map/jit(take_along_axis)/gather | solution.py:42
  246.4 2.7 select_select_fusion
  249.1 53.7 %all_to_all.27 = bf16[8,512,512]{1,2,0:T(8,128)(2,1)} all-to-all(bf16[8,512,512]{1,2,0:T(8,128)(2,1)S(1)} %select_select_fusion), channel_id=1, replica_groups=mesh['dp'=16,'group'=8] {'group'}, dimensions={0} | all-to-all | bytes 8388608 | tf_op jit(solution)/shard_map/all_to_all | solution.py:30
  302.9 133.6 %all-reduce.6.cloned.1.call-done = bf16[512,4096]{0,1:T(8,128)(2,1)} async-done(((bf16[512,4096]{0,1:T(8,128)(2,1)}), bf16[512,4096]{0,1:T(8,128)(2,1)}) %all-reduce.6.cloned.1.call-update) | async-done | bytes 4194320 | tf_op jit(solution)/shard_map/psum | solution.py:31
  436.5 5.8 fusion.4
  442.3 12.5 %convolution_bitcast_fusion = f32[1,512,4096]{2,1,0:T(8,128)} fusion(bf16[1,512,4096]{2,1,0:T(8,128)(2,1)} %param.10, bf16[512,4096]{0,1:T(8,128)(2,1)} %all-reduce.6.cloned.1.call-done, bf16[1,4096,512]{2,1,0:T(8,128)(2,1)} %param.9, f32[512,512]{1,0:T(8,128)S(1)} %fusion.4), kind=kOutput, calls=%fused_computation.6 | convolution fusion | flops 4296540160 | bytes 22020096 | tf_op jit(solution)/shard_map/ech,ehd->ecd/dot_general | solution.py:37
  454.8 177.6 %all-reduce.7 = bf16[1,512,4096]{2,1,0:T(8,128)(2,1)} all-reduce(f32[1,512,4096]{2,1,0:T(8,128)} %convolution_bitcast_fusion), channel_id=1, replica_groups=mesh['dp'=16,'group'=8] {'dp'}, use_global_device_ids=true, to_apply=%region_4.5 | all-reduce | flops 2097152 | bytes 12582912 | tf_op jit(solution)/shard_map/psum | solution.py:40
  632.4 18.9 %copy.15 = bf16[1,512,4096]{1,0,2:T(2,128)(2,1)} copy(bf16[1,512,4096]{2,1,0:T(8,128)(2,1)} %all-reduce.7) | data formatting | bytes 8388608 | tf_op jit(solution)/shard_map/convert_element_type | solution.py:40
  651.3 0.5 broadcast.70
  651.8 28.5 %reduce = bf16[4096,512]{1,0:T(8,128)(2,1)} reduce(bf16[4096,1,512]{2,1,0:T(2,128)(2,1)} %bitcast.64, bf16[]{:T(256)} %broadcast.70), dimensions={1}, to_apply=%bitcast.56.reduce_sub_computation | reduce | bytes 8388610
  680.2 7.8 reshape.140
  688.0 6.3 all-to-all-start.1
  694.3 46.9 %all-to-all-done.1 = bf16[8,2,131072]{2,1,0:T(2,128)(2,1)} async-done(((bf16[8,2,131072]{2,1,0:T(2,128)(2,1)}), bf16[8,2,131072]{2,1,0:T(2,128)(2,1)}, u32[]{:S(2)}, u32[]{:S(2)}) %all-to-all-start.1) | async-done | bytes 4194336 | tf_op jit(solution)/shard_map/all_to_all | solution.py:41
  741.3 8.8 %reshape.141 = bf16[4096,1,512]{2,1,0:T(2,128)(2,1)} reshape(bf16[8,2,131072]{2,1,0:T(2,128)(2,1)} %all-to-all-done.1) | data formatting | bytes 8388608
  750.1 20.8 %copy.16 = f32[1,512,8,512]{3,1,2,0:T(8,128)} copy(bf16[1,512,8,512]{1,0,3,2:T(2,128)(2,1)} %bitcast.65) | data formatting | bytes 12582912 | tf_op jit(solution)/shard_map/convert_element_type | solution.py:43
  770.8 8.9 %convert_select_fusion = f32[4096,512]{1,0:T(8,128)} fusion(f32[1,512,8,512]{3,1,2,0:T(8,128)} %copy.16, f32[4096]{0:T(1024)S(1)} %bitcast.72, pred[4096]{0:T(1024)(128)(4,1)S(1)} %bitcast.74), kind=kLoop, calls=%fused_computation.5 | loop fusion | flops 8388608 | bytes 16797696 | tf_op jit(solution)/shard_map/jit(_where)/select_n | solution.py:45
  779.7 30.4 %scatter_custom_fusion = f32[4096,512]{1,0:T(8,128)} fusion(s32[4096]{0:T(1024)S(1)} %bitcast.70, f32[4096,512]{1,0:T(8,128)} %convert_select_fusion, f32[]{:T(128)} %constant.15.clone.1), kind=kCustom, calls=%fused_computation.14 | custom fusion | flops 2097152 | bytes 8389120 | tf_op jit(solution)/shard_map/scatter-add | solution.py:46
  810.1 5.9 convert_element_type.41
  (18 shorter events, 0.2 us)
Async XLA Ops:
  6.5 1.0 copy-start
  6.5 194.7 %all-reduce.4.cloned.1.call-start = ((), (), s32[]{:S(2)}) async-start(), calls=%async_computation.2 | async-start | bytes 8388608 | tf_op jit(solution)/shard_map/psum | solution.py:17
  13.0 0.7 copy-start.3
  13.0 423.5 %all-reduce.6.cloned.1.call-start = ((), (), s32[]{:S(2)}) async-start(), calls=%async_computation.3 | async-start | bytes 8388608 | tf_op jit(solution)/shard_map/psum | solution.py:31
  204.1 3.5 copy-start.2
  688.0 53.3 %all-to-all-start.1 = ((bf16[8,2,131072]{2,1,0:T(2,128)(2,1)}), bf16[8,2,131072]{2,1,0:T(2,128)(2,1)}, u32[]{:S(2)}, u32[]{:S(2)}) async-start(bf16[8,2,131072]{2,1,0:T(2,128)(2,1)} %reshape.140), calls=%async_computation.1 | async-start | bytes 8388608 | tf_op jit(solution)/shard_map/all_to_all | solution.py:41
  779.7 36.3 %copy-start.1 = (f32[512,256]{1,0:T(8,128)S(1)}, f32[512,256]{1,0:T(8,128)}, u32[]{:S(2)}) copy-start(f32[512,256]{1,0:T(8,128)} %param.7) | copy-start | bytes 1572868
Sparse Core Ops, SparseCore 0:
  13.1 188.0 all-reduce.3
  303.0 133.4 all-reduce.5
where the time goes:
time: 830 us; the launch traced here: 823 us
  waiting for transfers between devices  341 us (41%)
  blocking collectives  231 us (28%)
  local copies, waits for them, and re-layouts  121 us (15%)
  other arithmetic  85.9 us (10%)
  matrix products  23.7 us (3%)
  between operations  13.5 us (2%)
    psum x1, blocking collectives, shards(): summed_out = lax.psum(partial_out, 'dp').astype(jnp.bfloat16)  178 us
    psum x1, waiting for transfers between devices, shards(): logits = lax.psum(partial_value, 'group')  161 us
    psum x1, waiting for transfers between devices, shards(): lax.psum(arrived, 'dp').astype(jnp.float32).astype(jnp.bfloat16)  134 us
    all_to_all x1, blocking collectives, shards(): lax.all_to_all(selected, 'group', split_axis=0, concat_axis=2, tiled=True)  53.7 us
    all_to_all x1, waiting for transfers between devices, shards(): lax.all_to_all(summed_out, 'group', split_axis=2, concat_axis=0, tiled=True)  46.9 us
    scatter-add x1, other arithmetic, shards(): jnp.zeros((tok_rows, feat_slice), jnp.float32).at[flat_idx].add(weighted)  30.4 us
    unnamed x4, other arithmetic  28.5 us
    gather x2, local copies, waits for them, and re-layouts, shards(): jnp.take_along_axis(chosen.T, safe_idx, axis=1)  27.6 us
  transfers between devices with their start and end apart: 3, of which 3 were waited for; matrix products, arithmetic and copies ran while one was open for 3% of the time, Pallas kernels for 0%

commit v1 on v0

v1 whole, which is shorter than its diff:
```python
import functools

import jax
import jax.numpy as jnp
from jax import lax
from jax.experimental import pallas as pl
from jax.experimental.pallas import tpu as pltpu
from jax.sharding import PartitionSpec as P

MESH = pl.DeviceIdType.MESH
BF16 = jnp.bfloat16
F32 = jnp.float32
DP = 16
GRP = 8
CAPS = (48, 256)
BLK = 256
ROWS = 32
HALF = 16


def iota(shape, dim, dtype=jnp.int32):
    out = lax.broadcasted_iota(jnp.int32, shape, dim)
    return out if dtype == jnp.int32 else out.astype(dtype)


def earlier(n):
    return jnp.where(iota((n, n), 0) < iota((n, n), 1), 1.0, 0.0).astype(BF16)


def expert_kernel(
    picks_ref, tok_hbm, wr_hbm, wg_hbm, wu_hbm, wd_hbm,
    back_ref, index_ref,
    tok, wr, wg, wu, wd, onehot, packed, arrived, spread, rows, logit_part, logit_all,
    x, hidden, part, core_in, h0_in, h1_in, h1_edge, weighted, returned, outgoing,
    load_sem, own_sem,
    tok_ss, tok_rs, row_ss, row_rs, log_ss, log_rs, ag_ss, ag_rs, sib_ss, sib_rs,
    core_ss, core_rs, rs_ss, rs_rs, ret_ss, ret_rs, out_ss, out_rs,
):
    cap = packed.shape[1]
    step_blocks = onehot.shape[0] // cap
    d, g = lax.axis_index("dp"), lax.axis_index("group")
    y, xl, core = d // 4, (d // 2) % 2, d % 2
    tok_rows = tok.shape[0]
    feats = tok.shape[1]

    def block(yy, xx, cc):
        return (yy * 2 + xx) * 2 + cc

    up, down, far = (y + 1) % 4, (y + 3) % 4, (y + 2) % 4
    ox, oc = 1 - xl, 1 - core
    to_up = (block(up, xl, core), g)
    to_down = (block(down, xl, core), g)
    to_x = (block(y, ox, core), g)
    to_core = (block(y, xl, oc), g)

    sent = []

    def remote(src, dst, ss, rs, device):
        return pltpu.make_async_remote_copy(
            src_ref=src, dst_ref=dst, send_sem=ss, recv_sem=rs, device_id=device, device_id_type=MESH
        )

    def send(src, dst, ss, rs, device):
        copy = remote(src, dst, ss, rs, device)
        copy.start()
        sent.append(copy)
        return copy

    loads = []
    for i, (src, dst) in enumerate(
        ((tok_hbm, tok), (wr_hbm, wr), (wg_hbm, wg), (wu_hbm, wu), (wd_hbm, wd))
    ):
        copy = pltpu.make_async_copy(src, dst, load_sem.at[i])
        copy.start()
        loads.append(copy)

    barrier = pltpu.get_barrier_semaphore()
    for k in range(1, DP):
        pl.semaphore_signal(barrier, inc=1, device_id=((d + k) % DP, g), device_id_type=MESH)
    for k in range(1, GRP):
        pl.semaphore_signal(barrier, inc=1, device_id=(d, (g + k) % GRP), device_id_type=MESH)

    tri = earlier(BLK)
    local = picks_ref[...] - d * tok_rows
    mine = (local >= 0) & (local < tok_rows)
    rank = jnp.dot(
        jnp.where(mine, 1.0, 0.0).astype(BF16), tri, preferred_element_type=F32
    )
    rank = jnp.where(mine, rank, -1.0)
    local = local.astype(F32)
    slot_rank = iota((cap, BLK), 0, F32)
    for b in range(DP):
        chosen = jnp.where(slot_rank == rank[b : b + 1, :], local[b : b + 1, :], -1.0)
        index = jnp.max(chosen, axis=1, keepdims=True)
        index_ref[pl.ds(b * cap, cap), :] = jnp.broadcast_to(index, (cap, 128))

    owner = picks_ref[pl.ds(d, 1), :] // tok_rows
    is_owner = jnp.where(iota((DP, BLK), 0) == owner, 1.0, 0.0)
    ranks = jnp.dot(is_owner.astype(BF16), tri, preferred_element_type=F32)
    place = jnp.sum(is_owner * ranks, axis=0, keepdims=True) + owner.astype(F32) * cap
    spread[...] = jnp.where(iota((DP * cap, BLK), 0, F32) == place, 1.0, 0.0).astype(BF16)

    loads[0].wait()
    pl.semaphore_wait(barrier, DP - 1 + GRP - 1)
    lanes = iota((step_blocks * cap, 128), 1, F32)

    def gather(step, carry):
        turn = step * step_blocks // 4
        yy = (y + jnp.where(turn == 2, 3, jnp.where(turn == 3, 0, 2 - turn))) % 4
        first = yy * 4 + step * step_blocks % 4
        index = index_ref[pl.ds(pl.multiple_of(first * cap, 16), step_blocks * cap), :]
        for t in range(tok_rows // 128):
            onehot[:, t * 128 : (t + 1) * 128] = jnp.where(
                index == lanes + float(t * 128), 1.0, 0.0
            ).astype(BF16)
        taken = jnp.dot(onehot[...], tok[...], preferred_element_type=F32).astype(BF16)
        packed[pl.ds(first, step_blocks)] = taken.reshape(step_blocks, cap, feats)
        for i in range(step_blocks):
            to = first + i
            k = (to - d + DP) % DP

            @pl.when(to != d)
            def _():
                remote(packed.at[to], arrived.at[d], tok_ss.at[k], tok_rs.at[k], (to, g)).start()

        return carry

    lax.fori_loop(0, DP // step_blocks, gather, 0)
    own = pltpu.make_async_copy(packed.at[d], arrived.at[d], own_sem.at[0])
    own.start()
    loads[1].wait()
    hi = wr[...].astype(BF16)
    lo = (wr[...] - hi.astype(F32)).astype(BF16)
    own.wait()
    for k in range(1, DP):
        frm = (d - k + DP) % DP
        remote(packed.at[frm], arrived.at[frm], tok_ss.at[k], tok_rs.at[k], (frm, g)).wait_recv()

    taken = lax.dot_general(
        spread[...], arrived[...].reshape(DP * cap, feats), (((0,), (0,)), ((), ())),
        preferred_element_type=F32,
    ).astype(BF16)
    rows[...] = taken.reshape(GRP, ROWS, feats)
    mine_cols = pl.ds(pl.multiple_of(g * feats, feats), feats)
    for k in range(1, GRP):
        q = (g + k) % GRP
        send(rows.at[q], x.at[d, :, mine_cols], row_ss.at[k], row_rs.at[k], (d, q))
    own = pltpu.make_async_copy(rows.at[g], x.at[d, :, mine_cols], own_sem.at[1])
    own.start()
    logits = jnp.dot(taken, hi, preferred_element_type=F32) + jnp.dot(
        taken, lo, preferred_element_type=F32
    )
    logit_part[...] = logits.reshape(GRP, ROWS, logits.shape[1])
    own.wait()
    for k in range(1, GRP):
        frm = (g - k + GRP) % GRP
        cols = pl.ds(pl.multiple_of(frm * feats, feats), feats)
        remote(rows.at[frm], x.at[d, :, cols], row_ss.at[k], row_rs.at[k], (d, frm)).wait_recv()

    h0, h1 = pl.ds(0, HALF), pl.ds(HALF, HALF)
    wide = x.shape[2]
    left, right = pl.ds(0, wide // 2), pl.ds(wide // 2, wide // 2)

    def ag(i, b, half, to, cols=None):
        ref = x.at[b, half] if cols is None else x.at[b, half, cols]
        return send(ref, ref, ag_ss.at[i], ag_rs.at[i], to)

    def got(i, b, half, cols=None):
        ref = x.at[b, half] if cols is None else x.at[b, half, cols]
        remote(ref, ref, ag_ss.at[i], ag_rs.at[i], to_x).wait_recv()

    n_sib = [0]

    def sib(b, half):
        ref = x.at[b, half]
        send(ref, ref, sib_ss.at[n_sib[0]], sib_rs.at[n_sib[0]], to_core)
        n_sib[0] += 1

    own_b, x_b = block(y, xl, core), block(y, ox, core)
    up_b, down_b, far_b = block(up, xl, core), block(down, xl, core), block(far, xl, core)
    up_x, down_x, far_x = block(up, ox, core), block(down, ox, core), block(far, ox, core)
    ag(0, own_b, h0, to_x)
    ag(7, own_b, h1, to_up)
    ag(8, own_b, h1, to_down)
    ag(1, own_b, h0, to_up)
    ag(2, own_b, h0, to_down)
    ag(9, own_b, h1, to_x)
    sib(own_b, h0)
    sib(own_b, h1)
    for k in range(1, GRP):
        q = (g + k) % GRP
        send(logit_part.at[q], logit_all.at[g], log_ss.at[k], log_rs.at[k], (d, q))
    own2 = pltpu.make_async_copy(logit_part.at[g], logit_all.at[g], own_sem.at[2])
    own2.start()
    got(0, x_b, h0)
    ag(3, x_b, h0, to_up)
    ag(4, x_b, h0, to_down)
    sib(x_b, h0)
    got(7, down_b, h1)
    ag(10, down_b, h1, to_up, left)
    ag(12, down_b, h1, to_x)
    sib(down_b, h1)
    got(8, up_b, h1)
    ag(11, up_b, h1, to_down, right)
    ag(13, up_b, h1, to_x)
    sib(up_b, h1)
    got(1, down_b, h0)
    ag(5, down_b, h0, to_up)
    sib(down_b, h0)
    got(2, up_b, h0)
    sib(up_b, h0)
    got(9, x_b, h1)
    sib(x_b, h1)
    got(4, up_x, h0)
    ag(6, up_x, h0, to_down)
    sib(up_x, h0)
    got(3, down_x, h0)
    sib(down_x, h0)
    got(10, far_b, h1, left)
    got(11, far_b, h1, right)
    ag(14, far_b, h1, to_x)
    sib(far_b, h1)
    got(12, down_x, h1)
    sib(down_x, h1)
    got(13, up_x, h1)
    sib(up_x, h1)
    got(5, far_b, h0)
    sib(far_b, h0)
    got(6, far_x, h0)
    sib(far_x, h0)
    got(14, far_x, h1)
    sib(far_x, h1)
    n_sib[0] = 0
    for i in range(16):
        ref = x.at[block(y, xl, oc), h0]
        remote(ref, ref, sib_ss.at[i], sib_rs.at[i], to_core).wait_recv()

    loads[2].wait()
    loads[3].wait()
    n_rows = DP * ROWS
    units = wg.shape[1]

    def into_hidden(step, carry):
        m = step // 2
        cols = pl.ds(pl.multiple_of((step % 2) * (units // 2), 128), units // 2)
        xs = x[pl.ds(m * 8, 8)].reshape(n_rows // 2, wide)
        gate = jnp.dot(xs, wg[:, cols], preferred_element_type=F32)
        lift = jnp.dot(xs, wu[:, cols], preferred_element_type=F32)
        value = gate / (1.0 + jnp.exp(-gate)) * lift
        hidden[pl.ds(pl.multiple_of(m * (n_rows // 2), 16), n_rows // 2), cols] = value.astype(BF16)
        return carry

    lax.fori_loop(0, 4, into_hidden, 0)
    loads[4].wait()

    def out_of_hidden(yy):
        hs = hidden[pl.ds(pl.multiple_of(yy * 4 * ROWS, 16), 4 * ROWS), :]

        def tile(step, carry):
            cols = pl.ds(pl.multiple_of(step * 512, 512), 512)
            value = jnp.dot(hs, wd[:, cols], preferred_element_type=F32).astype(BF16)
            part[pl.ds(yy * 4, 4), :, cols] = value.reshape(4, ROWS, 512)
            return carry

        lax.fori_loop(0, wide // 512, tile, 0)

    def to_sibling(i, yy):
        for xx in range(2):
            send(
                part.at[block(yy, xx, oc)], core_in.at[yy * 2 + xx],
                core_ss.at[2 * i + xx], core_rs.at[2 * i + xx], to_core,
            )

    def add_sibling(i, yy):
        for xx in range(2):
            b = block(yy, xx, core)
            remote(
                part.at[b], core_in.at[yy * 2 + xx],
                core_ss.at[2 * i + xx], core_rs.at[2 * i + xx], to_core,
            ).wait_recv()
            part[b] = (part[b].astype(F32) + core_in[yy * 2 + xx].astype(F32)).astype(BF16)

    def rs(i, src, dst, to):
        send(src, dst, rs_ss.at[i], rs_rs.at[i], to)

    def rs_got(i, dst):
        remote(dst, dst, rs_ss.at[i], rs_rs.at[i], to_x).wait_recv()

    def add(b, half, ref, cols=None):
        if cols is None:
            part[b, half] = (part[b, half].astype(F32) + ref[...].astype(F32)).astype(BF16)
        else:
            part[b, half, cols] = (part[b, half, cols].astype(F32) + ref[...].astype(F32)).astype(BF16)

    out_of_hidden(far)
    to_sibling(0, far)
    out_of_hidden(up)
    to_sibling(1, up)
    add_sibling(0, far)
    rs(0, part.at[far_b, h0], h0_in.at[0], to_up)
    rs(1, part.at[far_x, h0], h0_in.at[1], to_down)
    rs(7, part.at[far_x, h1], h1_in.at[0], to_x)
    out_of_hidden(down)
    to_sibling(2, down)
    add_sibling(1, up)
    rs(2, part.at[up_x, h0], h0_in.at[2], to_up)
    rs(8, part.at[up_x, h1], h1_in.at[1], to_x)
    rs_got(7, h1_in.at[0])
    add(far_b, h1, h1_in.at[0])
    rs(9, part.at[far_b, h1, left], h1_edge.at[0], to_up)
    rs(10, part.at[far_b, h1, right], h1_edge.at[1], to_down)
    out_of_hidden(y)
    to_sibling(3, y)
    add_sibling(2, down)
    rs(3, part.at[down_b, h0], h0_in.at[3], to_down)
    rs(11, part.at[down_x, h1], h1_in.at[2], to_x)
    rs_got(0, h0_in.at[0])
    add(up_b, h0, h0_in.at[0])
    rs(4, part.at[up_b, h0], h0_in.at[4], to_up)
    rs_got(1, h0_in.at[1])
    add(down_x, h0, h0_in.at[1])
    rs(5, part.at[down_x, h0], h0_in.at[5], to_down)
    rs_got(8, h1_in.at[1])
    add(up_b, h1, h1_in.at[1])
    rs_got(9, h1_edge.at[0])
    add(up_b, h1, h1_edge.at[0], left)
    rs(12, part.at[up_b, h1], h1_in.at[4], to_up)
    rs_got(11, h1_in.at[2])
    add(down_b, h1, h1_in.at[2])
    rs_got(10, h1_edge.at[1])
    add(down_b, h1, h1_edge.at[1], right)
    rs(13, part.at[down_b, h1], h1_in.at[5], to_down)
    add_sibling(3, y)
    rs(14, part.at[x_b, h1], h1_in.at[3], to_x)

    own2.wait()
    for k in range(1, GRP):
        frm = (g - k + GRP) % GRP
        remote(logit_part.at[frm], logit_all.at[frm], log_ss.at[k], log_rs.at[k], (d, frm)).wait_recv()
    logits = logit_all[0]
    for q in range(1, GRP):
        logits = logits + logit_all[q]
    n_exp = logits.shape[1]
    grown = jnp.exp(logits - jnp.max(logits, axis=1, keepdims=True))
    column = iota(logits.shape, 1) == g * (n_exp // GRP)
    prob = jnp.sum(jnp.where(column, grown, 0.0), axis=1, keepdims=True) / jnp.sum(
        grown, axis=1, keepdims=True
    )

    rs_got(2, h0_in.at[2])
    rs_got(5, h0_in.at[5])
    part[x_b, h0] = (
        part[x_b, h0].astype(F32) + h0_in[2].astype(F32) + h0_in[5].astype(F32)
    ).astype(BF16)
    rs(6, part.at[x_b, h0], h0_in.at[6], to_x)
    rs_got(3, h0_in.at[3])
    rs_got(4, h0_in.at[4])
    first = part[own_b, h0].astype(F32) + h0_in[3].astype(F32) + h0_in[4].astype(F32)
    rs_got(6, h0_in.at[6])
    first = (first + h0_in[6].astype(F32)).astype(BF16).astype(F32)
    weighted[h0] = (first * prob[:HALF]).astype(BF16)
    rs_got(14, h1_in.at[3])
    rs_got(12, h1_in.at[4])
    rs_got(13, h1_in.at[5])
    second = part[own_b, h1].astype(F32) + h1_in[3].astype(F32)
    second = second + h1_in[4].astype(F32) + h1_in[5].astype(F32)
    weighted[h1] = (second.astype(BF16).astype(F32) * prob[HALF:]).astype(BF16)

    for k in range(1, GRP):
        q = (g + k) % GRP
        cols = pl.ds(pl.multiple_of(q * feats, feats), feats)
        send(weighted.at[:, cols], returned.at[g], ret_ss.at[k], ret_rs.at[k], (d, q))
    own = pltpu.make_async_copy(weighted.at[:, mine_cols], returned.at[g], own_sem.at[3])
    own.start()
    own.wait()
    for k in range(1, GRP):
        frm = (g - k + GRP) % GRP
        remote(returned.at[frm], returned.at[frm], ret_ss.at[k], ret_rs.at[k], (d, frm)).wait_recv()

    back = jnp.dot(
        spread[...], returned[...].reshape(BLK, feats), preferred_element_type=F32
    ).astype(BF16)
    outgoing[...] = back.reshape(DP, cap, feats)
    for k in range(1, DP):
        to = (d + k) % DP
        send(outgoing.at[to], back_ref.at[d], out_ss.at[k], out_rs.at[k], (to, g))
    own = pltpu.make_async_copy(outgoing.at[d], back_ref.at[d], own_sem.at[4])
    own.start()
    own.wait()
    for k in range(1, DP):
        frm = (d - k + DP) % DP
        remote(outgoing.at[frm], back_ref.at[frm], out_ss.at[k], out_rs.at[k], (frm, g)).wait_recv()

    for k in range(1, DP):
        to = (d + k) % DP
        remote(packed.at[to], arrived.at[d], tok_ss.at[k], tok_rs.at[k], (to, g)).wait_send()
    for copy in sent:
        copy.wait_send()


def mix_kernel(index_ref, back_ref, out_ref, index_rows):
    tile = out_ref.shape[0]
    packed = index_ref.shape[0]

    @pl.when(pl.program_id(0) == 0)
    def _():
        index_rows[...] = index_ref[...].T

    first = (pl.program_id(0) * tile).astype(F32)
    parts = []
    for t in range(tile // 128):
        token = iota((128, packed), 0, F32) + (first + float(t * 128))
        parts.append(jnp.where(index_rows[...] == token, 1.0, 0.0).astype(BF16))
    onehot = jnp.concatenate(parts, axis=0)
    out_ref[...] = jnp.dot(onehot, back_ref[...], preferred_element_type=F32).astype(BF16)


def kernel_shards(tokens, router_weight, gate_weight, up_weight, down_weight, blocks, cap):
    packed = DP * cap
    step_rows = 4 * cap if cap < 64 else cap
    tok_rows, feats = tokens.shape
    units, wide = down_weight.shape[1:]
    n_exp = router_weight.shape[1]
    dma = pltpu.SemaphoreType.DMA
    any_spec = pl.BlockSpec(memory_space=pl.ANY)
    vmem_spec = pl.BlockSpec(memory_space=pltpu.VMEM)
    back, index = pl.pallas_call(
        expert_kernel,
        out_shape=(
            jax.ShapeDtypeStruct((DP, cap, feats), BF16),
            jax.ShapeDtypeStruct((packed, 128), F32),
        ),
        in_specs=[vmem_spec] + [any_spec] * 5,
        out_specs=(any_spec, vmem_spec),
        scratch_shapes=[
            pltpu.VMEM((tok_rows, feats), BF16),
            pltpu.VMEM((feats, n_exp), F32),
            pltpu.VMEM((wide, units), BF16),
            pltpu.VMEM((wide, units), BF16),
            pltpu.VMEM((units, wide), BF16),
            pltpu.VMEM((step_rows, tok_rows), BF16),
            pltpu.VMEM((DP, cap, feats), BF16),
            pltpu.VMEM((DP, cap, feats), BF16),
            pltpu.VMEM((packed, BLK), BF16),
            pltpu.VMEM((GRP, ROWS, feats), BF16),
            pltpu.VMEM((GRP, ROWS, n_exp), F32),
            pltpu.VMEM((GRP, ROWS, n_exp), F32),
            pltpu.VMEM((DP, ROWS, wide), BF16),
            pltpu.VMEM((DP * ROWS, units), BF16),
            pltpu.VMEM((DP, ROWS, wide), BF16),
            pltpu.VMEM((DP // 2, ROWS, wide), BF16),
            pltpu.VMEM((7, HALF, wide), BF16),
            pltpu.VMEM((6, HALF, wide), BF16),
            pltpu.VMEM((2, HALF, wide // 2), BF16),
            pltpu.VMEM((ROWS, wide), BF16),
            pltpu.VMEM((GRP, ROWS, feats), BF16),
            pltpu.VMEM((DP, cap, feats), BF16),
            dma((5,)),
            dma((5,)),
            dma((DP,)), dma((DP,)),
            dma((GRP,)), dma((GRP,)),
            dma((GRP,)), dma((GRP,)),
            dma((15,)), dma((15,)),
            dma((16,)), dma((16,)),
            dma((8,)), dma((8,)),
            dma((15,)), dma((15,)),
            dma((GRP,)), dma((GRP,)),
            dma((DP,)), dma((DP,)),
        ],
        compiler_params=pltpu.CompilerParams(
            collective_id=cap, has_side_effects=True, vmem_limit_bytes=60 * 2**20
        ),
        cost_estimate=pl.CostEstimate(
            flops=11 * 10**9, bytes_accessed=18 * 2**20, transcendentals=512 * 512
        ),
        name="experts",
    )(
        blocks, tokens, router_weight, gate_weight[0], up_weight[0], down_weight[0]
    )
    tile = 512
    return pl.pallas_call(
        mix_kernel,
        grid=(tok_rows // tile,),
        out_shape=jax.ShapeDtypeStruct((tok_rows, feats), BF16),
        in_specs=[
            pl.BlockSpec((packed, 128), lambda i: (0, 0)),
            pl.BlockSpec((packed, feats), lambda i: (0, 0)),
        ],
        out_specs=pl.BlockSpec((tile, feats), lambda i: (i, 0)),
        scratch_shapes=[pltpu.VMEM((128, packed), F32)],
        compiler_params=pltpu.CompilerParams(vmem_limit_bytes=60 * 2**20),
        cost_estimate=pl.CostEstimate(
            flops=2 * tok_rows * packed * feats, bytes_accessed=6 * 2**20, transcendentals=0
        ),
        name="mix",
    )(index, back.reshape(packed, feats))


def shards(tokens, router_weight, gate_weight, up_weight, down_weight, picks):
    tok_rows = tokens.shape[0]
    flight, capacity = picks.shape
    blocks = picks.reshape(flight, DP, ROWS).transpose(1, 0, 2).reshape(DP, BLK)
    owners = blocks // tok_rows
    counts = jnp.sum(
        (owners[:, None, :] == jnp.arange(DP)[None, :, None]).astype(jnp.int32), axis=2
    )
    fits = jnp.max(counts) <= CAPS[0]
    args = (tokens, router_weight, gate_weight, up_weight, down_weight, blocks)
    return lax.cond(fits, lambda: kernel_shards(*args, CAPS[0]), lambda: kernel_shards(*args, CAPS[1]))


def solution(mesh):
    in_specs = (
        P("dp", "group"),
        P("group", None),
        P("group", None, "dp"),
        P("group", None, "dp"),
        P("group", "dp", None),
        P(),
    )
    out_specs = P("dp", "group")
    return jax.shard_map(shards, mesh=mesh, in_specs=in_specs, out_specs=out_specs, check_vma=False)
```

time: 830 us -> 103 us (0.12)
  waiting for transfers between devices: 341 us -> 0 us
  blocking collectives: 231 us -> 0 us
  local copies, waits for them, and re-layouts: 121 us -> 0.9 us
  Pallas kernels: 0 us -> 100 us
  other arithmetic: 85.9 us -> 1 us
  matrix products: 23.7 us -> 0 us
  between operations: 13.5 us -> 0.68 us
    psum x2 -> x0, waiting for transfers between devices: 294 us -> none  [the longest x1 161 us: shards(): logits = lax.psum(partial_value, 'group')]
    psum x1 -> x0, blocking collectives: 178 us -> none  [shards(): summed_out = lax.psum(partial_out, 'dp').astype(jnp.bfloat16)]
    pallas_call x0 -> x2, Pallas kernels: none -> 100 us  [the longest x1 92.9 us: kernel_shards(): pl.pallas_call(expert_kernel, out_shape=(jax.ShapeDtypeStruct((DP, cap, f...]
    gather x4 -> x0, local copies, waits for them, and re-layouts: 54.3 us -> none  [the longest x2 27.6 us: shards(): jnp.take_along_axis(chosen.T, safe_idx, axis=1)]
    all_to_all x1 -> x0, blocking collectives: 53.7 us -> none  [shards(): lax.all_to_all(selected, 'group', split_axis=0, concat_axis=2, tiled=True)]
    all_to_all x1 -> x0, waiting for transfers between devices: 46.9 us -> none  [shards(): lax.all_to_all(summed_out, 'group', split_axis=2, concat_axis=0, tiled=True)]
    convert_element_type x2 -> x0, local copies, waits for them, and re-layouts: 39.6 us -> none  [the longest x1 20.8 us: shards(): returned.astype(jnp.float32)]
    scatter-add x1 -> x0, other arithmetic: 30.4 us -> none  [shards(): jnp.zeros((tok_rows, feat_slice), jnp.float32).at[flat_idx].add(weighted)]
  transfers between devices with their start and end apart: 3 -> 0, of which waited for: 3 -> 0; matrix products, arithmetic and copies ran while one was open for 3% -> 0% of each run, Pallas kernels for 0% -> 0%
where the time goes in v1:
time: 103 us
  Pallas kernels  100 us (97%)
    pallas_call x1, Pallas kernels, kernel_shards(): pl.pallas_call(expert_kernel, out_shape=(jax.ShapeDtypeStruct((DP, cap, f...  92.9 us
    pallas_call x1, Pallas kernels, kernel_shards(): pl.pallas_call(mix_kernel, grid=(tok_rows // tile,), out_shape=jax.ShapeD...  7.5 us

profile of v1, /device:TPU:1, one launch (start us, length us, event | category | flops | bytes accessed | tf_op | source)
XLA Modules:
  0.0 103.1 jit_solution(14585750796246291084)
XLA Ops:
  0.0 0.8 reshape.40
  0.8 0.1 reshape.41
  0.9 0.3 convert_reduce_fusion
  1.3 0.6 reduce_max.9
  2.6 100.6 %conditional.1 = (bf16[4096,512]{1,0:T(8,128)(2,1)}) conditional(s32[]{:T(128)} %convert_element_type.7, (bf16[1,4096,512]{2,1,0:T(8,128)(2,1)}, bf16[1,4096,512]{2,1,0:T(8,128)(2,1)}, bf16[1,512,4096]{2,1,0:T(8,128)(2,1)}, s32[16,256]{1,0:T(8,128)S(1)}, bf16[4096,512]{1,0:T(8,128)(2,1)}, /*index=5*/f32[512,256]{1,0:T(8,128)}) %tuple.11, ...), branch_computations={%region_2.3_spmd, %region_3.4_spmd} | conditional | flops 28179869696 | bytes 25165832 | solution.py:509
  2.8 92.9 %experts.3 = (bf16[16,48,512]{2,1,0:T(8,128)(2,1)}, f32[768,128]{1,0:T(8,128)}) custom-call(s32[16,256]{1,0:T(8,128)S(1)} %get-tuple-element.40.picks_ref, bf16[4096,512]{1,0:T(8,128)(2,1)} %get-tuple-element.41.tok_hbm, f32[512,256]{1,0:T(8,128)} %get-tuple-element.42.wr_hbm, bf16[4096,512]{1,0:T(8,128)(2,1)} %bitcast.13, bf16[4096,512]{1,0:T(8,128)(2,1)} %bitcast.15, ...), custom_call_target="tpu_custom_call" | custom-call | flops 11000000512 | bytes 18874368 | tf_op jit(solution)/shard_map/cond/branch_1_fun/experts/pallas_call | solution.py:427
  95.6 7.5 %mix.3 = bf16[4096,512]{1,0:T(8,128)(2,1)} custom-call(f32[768,128]{1,0:T(8,128)} %get-tuple-element.46.index_ref, bf16[768,512]{1,0:T(8,128)(2,1)} %bitcast.19), custom_call_target="tpu_custom_call" | custom-call | flops 3221225472 | bytes 6291456 | tf_op jit(solution)/shard_map/cond/branch_1_fun/mix/pallas_call | solution.py:481
  (2 shorter events, 0.0 us)

commit v2 on v1

--- a/solution.py
+++ b/solution.py
@@ -12,7 +12,7 @@
 F32 = jnp.float32
 DP = 16
 GRP = 8
-CAPS = (48, 256)
+NEAR = 16
 BLK = 256
 ROWS = 32
 HALF = 16
@@ -24,12 +24,114 @@
 
 
 def earlier(n):
-    return jnp.where(iota((n, n), 0) < iota((n, n), 1), 1.0, 0.0).astype(BF16)
+    return ones(iota((n, n), 0) < iota((n, n), 1))
+
+
+def ones(mask):
+    return jnp.where(mask, 1.0, 0.0).astype(BF16)
+
+
+def mm(a, b):
+    return jnp.dot(a, b, preferred_element_type=F32)
+
+
+def over(values):
+    return jnp.sum(values, axis=0, keepdims=True)
+
+
+def best(hit, value):
+    return jnp.max(jnp.where(hit, value, -1.0), axis=1, keepdims=True)
+
+
+def fill_onehot(onehot, index):
+    rows = index.shape[0]
+    high = jnp.floor(index * (1.0 / 128.0))
+    lane = iota((rows, 128), 1, F32)
+    low = ones(index - high * 128.0 == lane)
+    high = high.astype(BF16)
+    for t in range(onehot.shape[1] // 128):
+        onehot[:, t * 128 : (t + 1) * 128] = jnp.where(high == float(t), low, 0.0).astype(BF16)
+
+
+def place_picks(picks_ref, me, tok_rows, index_ref, spread, fit_ref):
+    flight, cap = picks_ref.shape
+    n_pair = flight * DP
+    tri = earlier(cap)
+    picks = picks_ref[...]
+    owner = picks // tok_rows
+    local = (picks - owner * tok_rows).astype(F32)
+    dev = iota((DP, cap), 0)
+    dev_f = dev.astype(F32)
+    at_me = dev == me
+    owned = [ones(dev == owner[q : q + 1]) for q in range(flight)]
+    stacked = jnp.concatenate(owned, axis=0)
+    owned = [o.astype(F32) for o in owned]
+    before = mm(stacked, tri)
+    count = mm(stacked, jnp.full((cap, cap), 1.0, BF16))
+    room = jnp.maximum(ROWS - count, 0.0)
+    r, c = iota((n_pair, n_pair), 0), iota((n_pair, n_pair), 1)
+    turn = 2 * (r // DP) + 1
+    in_turn = (c + DP - turn % DP) % DP < (r + DP - turn % DP) % DP
+    room_before = mm(ones((r // DP == c // DP) & in_turn), room.astype(BF16))
+    earlier_expert = ones((r % DP == c % DP) & (c // DP < r // DP))
+
+    def of(values, q):
+        return values[q * DP : (q + 1) * DP]
+
+    rank = [over(owned[q] * of(before, q)) for q in range(flight)]
+    extra = [rank[q] >= ROWS for q in range(flight)]
+    extra_no = mm(jnp.concatenate([ones(e) for e in extra], axis=0), tri)
+    mine = [owner[q : q + 1] == me for q in range(flight)]
+    sends, takes, to_me, fits = [], [], [], jnp.zeros((DP, DP), F32)
+    for q in range(flight):
+        no = extra_no[q : q + 1]
+        first = of(room_before, q)
+        dest = jnp.where(
+            extra[q] & (no >= first) & (no < first + of(room, q)), 1.0, 0.0
+        )
+        to_me.append(over(jnp.where(at_me, dest, 0.0)))
+        sends.append(jnp.where(mine[q], dest, 0.0).astype(BF16))
+        takes.append((owned[q] * to_me[q]).astype(BF16))
+        fits = fits + lax.dot_general(
+            owned[q].astype(BF16), dest.astype(BF16), (((1,), (1,)), ((), ())),
+            preferred_element_type=F32,
+        )
+    fit_ref[...] = jnp.broadcast_to(jnp.max(fits, axis=(0, 1), keepdims=True), fit_ref.shape)
+
+    def keys(hits):
+        hits = jnp.concatenate(hits, axis=0)
+        counts = mm(hits, jnp.full((cap, cap), 1.0, BF16)).astype(BF16)
+        number = mm(hits, tri) + mm(earlier_expert, counts)
+        hits = hits.astype(F32)
+        return [over(of(hits, q) * (of(number, q) + NEAR * dev_f)) for q in range(flight)]
+
+    n_far = DP * NEAR
+    send_key, take_key = keys(sends), keys(takes)
+    slot = iota((n_far, cap), 0, F32)
+    far = jnp.full((n_far, cap), -1.0, F32)
+    for q in range(flight):
+        key = jnp.where(mine[q] & extra[q], send_key[q], -1.0)
+        far = jnp.where(slot == key, local[q : q + 1], far)
+    far = jnp.max(far, axis=1, keepdims=True)
+    index_ref[pl.ds(BLK, n_far), :] = jnp.broadcast_to(far, (n_far, 128))
+    slot = iota((ROWS, cap), 0, F32)
+    column = iota((ROWS, n_far), 1, F32)
+    for q in range(flight):
+        key = jnp.where(mine[q], rank[q], -1.0)
+        own = best(slot == key, local[q : q + 1])
+        index_ref[pl.ds(q * ROWS, ROWS), :] = jnp.broadcast_to(own, (ROWS, 128))
+        place = extra_no[q : q + 1] + over(
+            jnp.where(at_me, of(count, q) - of(room_before, q), 0.0)
+        )
+        place = jnp.where(to_me[q] > 0.0, place, -1.0)
+        source = best(slot == place, take_key[q])
+        spread[pl.ds(q * ROWS, ROWS), :] = ones(source == column)
 
 
 def expert_kernel(
+    quick,
     picks_ref, tok_hbm, wr_hbm, wg_hbm, wu_hbm, wd_hbm,
-    back_ref, index_ref,
+    back_ref, index_ref, fit_ref,
     tok, wr, wg, wu, wd, onehot, packed, arrived, spread, rows, logit_part, logit_all,
     x, hidden, part, core_in, h0_in, h1_in, h1_edge, weighted, returned, outgoing,
     load_sem, own_sem,
@@ -37,7 +139,6 @@
     core_ss, core_rs, rs_ss, rs_rs, ret_ss, ret_rs, out_ss, out_rs,
 ):
     cap = packed.shape[1]
-    step_blocks = onehot.shape[0] // cap
     d, g = lax.axis_index("dp"), lax.axis_index("group")
     y, xl, core = d // 4, (d // 2) % 2, d % 2
     tok_rows = tok.shape[0]
@@ -80,66 +181,73 @@
     for k in range(1, GRP):
         pl.semaphore_signal(barrier, inc=1, device_id=(d, (g + k) % GRP), device_id_type=MESH)
 
-    tri = earlier(BLK)
-    local = picks_ref[...] - d * tok_rows
-    mine = (local >= 0) & (local < tok_rows)
-    rank = jnp.dot(
-        jnp.where(mine, 1.0, 0.0).astype(BF16), tri, preferred_element_type=F32
-    )
-    rank = jnp.where(mine, rank, -1.0)
-    local = local.astype(F32)
-    slot_rank = iota((cap, BLK), 0, F32)
-    for b in range(DP):
-        chosen = jnp.where(slot_rank == rank[b : b + 1, :], local[b : b + 1, :], -1.0)
-        index = jnp.max(chosen, axis=1, keepdims=True)
-        index_ref[pl.ds(b * cap, cap), :] = jnp.broadcast_to(index, (cap, 128))
-
-    owner = picks_ref[pl.ds(d, 1), :] // tok_rows
-    is_owner = jnp.where(iota((DP, BLK), 0) == owner, 1.0, 0.0)
-    ranks = jnp.dot(is_owner.astype(BF16), tri, preferred_element_type=F32)
-    place = jnp.sum(is_owner * ranks, axis=0, keepdims=True) + owner.astype(F32) * cap
-    spread[...] = jnp.where(iota((DP * cap, BLK), 0, F32) == place, 1.0, 0.0).astype(BF16)
+    if quick:
+        place_picks(picks_ref, d, tok_rows, index_ref, spread, fit_ref)
+    else:
+        tri = earlier(BLK)
+        local = picks_ref[...] - d * tok_rows
+        mine = (local >= 0) & (local < tok_rows)
+        rank = jnp.dot(
+            jnp.where(mine, 1.0, 0.0).astype(BF16), tri, preferred_element_type=F32
+        )
+        rank = jnp.where(mine, rank, -1.0)
+        local = local.astype(F32)
+        slot_rank = iota((cap, BLK), 0, F32)
+        for b in range(DP):
+            chosen = jnp.where(slot_rank == rank[b : b + 1, :], local[b : b + 1, :], -1.0)
+            index = jnp.max(chosen, axis=1, keepdims=True)
+            index_ref[pl.ds(b * cap, cap), :] = jnp.broadcast_to(index, (cap, 128))
+
+        owner = picks_ref[pl.ds(d, 1), :] // tok_rows
+        is_owner = jnp.where(iota((DP, BLK), 0) == owner, 1.0, 0.0)
+        ranks = jnp.dot(is_owner.astype(BF16), tri, preferred_element_type=F32)
+        place = jnp.sum(is_owner * ranks, axis=0, keepdims=True) + owner.astype(F32) * cap
+        spread[...] = jnp.where(iota((DP * cap, BLK), 0, F32) == place, 1.0, 0.0).astype(BF16)
+        fit_ref[...] = jnp.zeros_like(fit_ref)
 
     loads[0].wait()
     pl.semaphore_wait(barrier, DP - 1 + GRP - 1)
-    lanes = iota((step_blocks * cap, 128), 1, F32)
-
-    def gather(step, carry):
-        turn = step * step_blocks // 4
-        yy = (y + jnp.where(turn == 2, 3, jnp.where(turn == 3, 0, 2 - turn))) % 4
-        first = yy * 4 + step * step_blocks % 4
-        index = index_ref[pl.ds(pl.multiple_of(first * cap, 16), step_blocks * cap), :]
-        for t in range(tok_rows // 128):
-            onehot[:, t * 128 : (t + 1) * 128] = jnp.where(
-                index == lanes + float(t * 128), 1.0, 0.0
-            ).astype(BF16)
-        taken = jnp.dot(onehot[...], tok[...], preferred_element_type=F32).astype(BF16)
-        packed[pl.ds(first, step_blocks)] = taken.reshape(step_blocks, cap, feats)
-        for i in range(step_blocks):
-            to = first + i
-            k = (to - d + DP) % DP
-
-            @pl.when(to != d)
+    if quick:
+        fill_onehot(onehot, index_ref[pl.ds(BLK, DP * cap), :])
+        packed[...] = mm(onehot[...], tok[...]).astype(BF16).reshape(DP, cap, feats)
+        for k in range(1, DP):
+            to = (d + k) % DP
+            send(packed.at[to], arrived.at[d], tok_ss.at[k], tok_rs.at[k], (to, g))
+        arrived[d] = jnp.zeros((cap, feats), BF16)
+        fill_onehot(onehot, index_ref[pl.ds(0, BLK), :])
+        kept = mm(onehot[...], tok[...])
+    else:
+
+        def gather(step, carry):
+            first = (d + 1 + step) % DP
+            fill_onehot(onehot, index_ref[pl.ds(pl.multiple_of(first * cap, 16), cap), :])
+            packed[first] = mm(onehot[...], tok[...]).astype(BF16)
+            k = (first - d + DP) % DP
+
+            @pl.when(first != d)
             def _():
-                remote(packed.at[to], arrived.at[d], tok_ss.at[k], tok_rs.at[k], (to, g)).start()
-
-        return carry
-
-    lax.fori_loop(0, DP // step_blocks, gather, 0)
-    own = pltpu.make_async_copy(packed.at[d], arrived.at[d], own_sem.at[0])
-    own.start()
+                remote(packed.at[first], arrived.at[d], tok_ss.at[k], tok_rs.at[k], (first, g)).start()
+
+            return carry
+
+        lax.fori_loop(0, DP, gather, 0)
+        own = pltpu.make_async_copy(packed.at[d], arrived.at[d], own_sem.at[0])
+        own.start()
+        own.wait()
     loads[1].wait()
     hi = wr[...].astype(BF16)
     lo = (wr[...] - hi.astype(F32)).astype(BF16)
-    own.wait()
     for k in range(1, DP):
         frm = (d - k + DP) % DP
         remote(packed.at[frm], arrived.at[frm], tok_ss.at[k], tok_rs.at[k], (frm, g)).wait_recv()
 
-    taken = lax.dot_general(
-        spread[...], arrived[...].reshape(DP * cap, feats), (((0,), (0,)), ((), ())),
-        preferred_element_type=F32,
-    ).astype(BF16)
+    came = arrived[...].reshape(DP * cap, feats)
+    if quick:
+        taken = (mm(spread[...], came) + kept).astype(BF16)
+    else:
+        taken = lax.dot_general(
+            spread[...], came, (((0,), (0,)), ((), ())), preferred_element_type=F32
+        ).astype(BF16)
     rows[...] = taken.reshape(GRP, ROWS, feats)
     mine_cols = pl.ds(pl.multiple_of(g * feats, feats), feats)
     for k in range(1, GRP):
@@ -366,82 +474,101 @@
     second = second + h1_in[4].astype(F32) + h1_in[5].astype(F32)
     weighted[h1] = (second.astype(BF16).astype(F32) * prob[HALF:]).astype(BF16)
 
+    mine_rows = pl.ds(pl.multiple_of(g * ROWS, ROWS), ROWS)
     for k in range(1, GRP):
         q = (g + k) % GRP
         cols = pl.ds(pl.multiple_of(q * feats, feats), feats)
-        send(weighted.at[:, cols], returned.at[g], ret_ss.at[k], ret_rs.at[k], (d, q))
-    own = pltpu.make_async_copy(weighted.at[:, mine_cols], returned.at[g], own_sem.at[3])
+        send(weighted.at[:, cols], returned.at[mine_rows], ret_ss.at[k], ret_rs.at[k], (d, q))
+    own = pltpu.make_async_copy(weighted.at[:, mine_cols], returned.at[mine_rows], own_sem.at[3])
     own.start()
     own.wait()
     for k in range(1, GRP):
         frm = (g - k + GRP) % GRP
-        remote(returned.at[frm], returned.at[frm], ret_ss.at[k], ret_rs.at[k], (d, frm)).wait_recv()
-
-    back = jnp.dot(
-        spread[...], returned[...].reshape(BLK, feats), preferred_element_type=F32
-    ).astype(BF16)
-    outgoing[...] = back.reshape(DP, cap, feats)
+        frm_rows = returned.at[pl.ds(pl.multiple_of(frm * ROWS, ROWS), ROWS)]
+        remote(frm_rows, frm_rows, ret_ss.at[k], ret_rs.at[k], (d, frm)).wait_recv()
+
+    block_rows = returned[...]
+    if quick:
+        base = BLK
+        kept_home = pltpu.make_async_copy(returned, back_ref.at[pl.ds(0, BLK)], own_sem.at[1])
+        kept_home.start()
+        back = lax.dot_general(
+            spread[...], block_rows, (((0,), (0,)), ((), ())), preferred_element_type=F32
+        )
+    else:
+        base = 0
+        back = mm(spread[...], block_rows)
+    outgoing[...] = back.astype(BF16).reshape(DP, cap, feats)
+    to_rows = back_ref.at[pl.ds(pl.multiple_of(base + d * cap, 16), cap)]
     for k in range(1, DP):
         to = (d + k) % DP
-        send(outgoing.at[to], back_ref.at[d], out_ss.at[k], out_rs.at[k], (to, g))
-    own = pltpu.make_async_copy(outgoing.at[d], back_ref.at[d], own_sem.at[4])
+        send(outgoing.at[to], to_rows, out_ss.at[k], out_rs.at[k], (to, g))
+    own = pltpu.make_async_copy(outgoing.at[d], to_rows, own_sem.at[4])
     own.start()
     own.wait()
+    if quick:
+        kept_home.wait()
     for k in range(1, DP):
         frm = (d - k + DP) % DP
-        remote(outgoing.at[frm], back_ref.at[frm], out_ss.at[k], out_rs.at[k], (frm, g)).wait_recv()
-
-    for k in range(1, DP):
-        to = (d + k) % DP
-        remote(packed.at[to], arrived.at[d], tok_ss.at[k], tok_rs.at[k], (to, g)).wait_send()
+        frm_rows = back_ref.at[pl.ds(pl.multiple_of(base + frm * cap, 16), cap)]
+        remote(outgoing.at[frm], frm_rows, out_ss.at[k], out_rs.at[k], (frm, g)).wait_recv()
+
+    if not quick:
+        for k in range(1, DP):
+            to = (d + k) % DP
+            remote(packed.at[to], arrived.at[d], tok_ss.at[k], tok_rs.at[k], (to, g)).wait_send()
     for copy in sent:
         copy.wait_send()
 
 
-def mix_kernel(index_ref, back_ref, out_ref, index_rows):
+def mix_kernel(index_ref, back_ref, out_ref, high, low):
     tile = out_ref.shape[0]
-    packed = index_ref.shape[0]
 
     @pl.when(pl.program_id(0) == 0)
     def _():
-        index_rows[...] = index_ref[...].T
-
-    first = (pl.program_id(0) * tile).astype(F32)
-    parts = []
-    for t in range(tile // 128):
-        token = iota((128, packed), 0, F32) + (first + float(t * 128))
-        parts.append(jnp.where(index_rows[...] == token, 1.0, 0.0).astype(BF16))
-    onehot = jnp.concatenate(parts, axis=0)
-    out_ref[...] = jnp.dot(onehot, back_ref[...], preferred_element_type=F32).astype(BF16)
-
-
-def kernel_shards(tokens, router_weight, gate_weight, up_weight, down_weight, blocks, cap):
+        index = index_ref[...].T
+        top = jnp.floor(index * (1.0 / 128.0))
+        high[...] = top.astype(BF16)
+        low[...] = ones(index - top * 128.0 == iota(index.shape, 0, F32))
+
+    first = (pl.program_id(0) * (tile // 128)).astype(F32)
+    like = (1, high.shape[1])
+    parts = [
+        jnp.where(high[...] == jnp.full(like, first + float(t), F32).astype(BF16), low[...], 0.0)
+        for t in range(tile // 128)
+    ]
+    out_ref[...] = mm(jnp.concatenate(parts, axis=0), back_ref[...]).astype(BF16)
+
+
+def route(tokens, router_weight, gate_weight, up_weight, down_weight, picks, quick):
+    cap = NEAR if quick else BLK
     packed = DP * cap
-    step_rows = 4 * cap if cap < 64 else cap
+    n_back = packed + (BLK if quick else 0)
     tok_rows, feats = tokens.shape
     units, wide = down_weight.shape[1:]
     n_exp = router_weight.shape[1]
     dma = pltpu.SemaphoreType.DMA
     any_spec = pl.BlockSpec(memory_space=pl.ANY)
     vmem_spec = pl.BlockSpec(memory_space=pltpu.VMEM)
-    back, index = pl.pallas_call(
-        expert_kernel,
+    return pl.pallas_call(
+        functools.partial(expert_kernel, quick),
         out_shape=(
-            jax.ShapeDtypeStruct((DP, cap, feats), BF16),
-            jax.ShapeDtypeStruct((packed, 128), F32),
+            jax.ShapeDtypeStruct((n_back, feats), BF16),
+            jax.ShapeDtypeStruct((n_back, 128), F32),
+            jax.ShapeDtypeStruct((8, 128), F32),
         ),
         in_specs=[vmem_spec] + [any_spec] * 5,
-        out_specs=(any_spec, vmem_spec),
+        out_specs=(any_spec, vmem_spec, vmem_spec),
         scratch_shapes=[
             pltpu.VMEM((tok_rows, feats), BF16),
             pltpu.VMEM((feats, n_exp), F32),
             pltpu.VMEM((wide, units), BF16),
             pltpu.VMEM((wide, units), BF16),
             pltpu.VMEM((units, wide), BF16),
-            pltpu.VMEM((step_rows, tok_rows), BF16),
+            pltpu.VMEM((BLK, tok_rows), BF16),
             pltpu.VMEM((DP, cap, feats), BF16),
             pltpu.VMEM((DP, cap, feats), BF16),
-            pltpu.VMEM((packed, BLK), BF16),
+            pltpu.VMEM((BLK, packed) if quick else (packed, BLK), BF16),
             pltpu.VMEM((GRP, ROWS, feats), BF16),
             pltpu.VMEM((GRP, ROWS, n_exp), F32),
             pltpu.VMEM((GRP, ROWS, n_exp), F32),
@@ -453,7 +580,7 @@
             pltpu.VMEM((6, HALF, wide), BF16),
             pltpu.VMEM((2, HALF, wide // 2), BF16),
             pltpu.VMEM((ROWS, wide), BF16),
-            pltpu.VMEM((GRP, ROWS, feats), BF16),
+            pltpu.VMEM((BLK, feats), BF16),
             pltpu.VMEM((DP, cap, feats), BF16),
             dma((5,)),
             dma((5,)),
@@ -468,45 +595,50 @@
             dma((DP,)), dma((DP,)),
         ],
         compiler_params=pltpu.CompilerParams(
-            collective_id=cap, has_side_effects=True, vmem_limit_bytes=60 * 2**20
+            collective_id=1 if quick else 2, has_side_effects=True, vmem_limit_bytes=60 * 2**20
         ),
         cost_estimate=pl.CostEstimate(
             flops=11 * 10**9, bytes_accessed=18 * 2**20, transcendentals=512 * 512
         ),
-        name="experts",
+        name="experts" if quick else "experts_any",
     )(
-        blocks, tokens, router_weight, gate_weight[0], up_weight[0], down_weight[0]
+        picks, tokens, router_weight, gate_weight[0], up_weight[0], down_weight[0]
     )
+
+
+def mix(back, index, tok_rows):
+    rows, feats = back.shape
     tile = 512
     return pl.pallas_call(
         mix_kernel,
         grid=(tok_rows // tile,),
         out_shape=jax.ShapeDtypeStruct((tok_rows, feats), BF16),
         in_specs=[
-            pl.BlockSpec((packed, 128), lambda i: (0, 0)),
-            pl.BlockSpec((packed, feats), lambda i: (0, 0)),
+            pl.BlockSpec((rows, 128), lambda i: (0, 0)),
+            pl.BlockSpec((rows, feats), lambda i: (0, 0)),
         ],
         out_specs=pl.BlockSpec((tile, feats), lambda i: (i, 0)),
-        scratch_shapes=[pltpu.VMEM((128, packed), F32)],
+        scratch_shapes=[pltpu.VMEM((128, rows), BF16), pltpu.VMEM((128, rows), BF16)],
         compiler_params=pltpu.CompilerParams(vmem_limit_bytes=60 * 2**20),
         cost_estimate=pl.CostEstimate(
-            flops=2 * tok_rows * packed * feats, bytes_accessed=6 * 2**20, transcendentals=0
+            flops=2 * tok_rows * rows * feats, bytes_accessed=6 * 2**20, transcendentals=0
         ),
         name="mix",
-    )(index, back.reshape(packed, feats))
+    )(index, back)
 
 
 def shards(tokens, router_weight, gate_weight, up_weight, down_weight, picks):
     tok_rows = tokens.shape[0]
     flight, capacity = picks.shape
-    blocks = picks.reshape(flight, DP, ROWS).transpose(1, 0, 2).reshape(DP, BLK)
-    owners = blocks // tok_rows
-    counts = jnp.sum(
-        (owners[:, None, :] == jnp.arange(DP)[None, :, None]).astype(jnp.int32), axis=2
-    )
-    fits = jnp.max(counts) <= CAPS[0]
-    args = (tokens, router_weight, gate_weight, up_weight, down_weight, blocks)
-    return lax.cond(fits, lambda: kernel_shards(*args, CAPS[0]), lambda: kernel_shards(*args, CAPS[1]))
+    args = (tokens, router_weight, gate_weight, up_weight, down_weight)
+    back, index, fit = route(*args, picks, True)
+
+    def any_picks():
+        blocks = picks.reshape(flight, DP, ROWS).transpose(1, 0, 2).reshape(DP, BLK)
+        back, index, _ = route(*args, blocks, False)
+        return mix(back, index, tok_rows)
+
+    return lax.cond(fit[0, 0] <= NEAR, lambda: mix(back, index, tok_rows), any_picks)
 
 
 def solution(mesh):

time: 103 us -> 92.1 us (0.89)
  Pallas kernels: 100 us -> 89.8 us
    pallas_call x2, Pallas kernels: 100 us -> 89.8 us  [the longest x1 84.3 us: route(): pl.pallas_call(functools.partial(expert_kernel, quick), out_shape=(jax.Sh...]
    slice x0 -> x1, local copies, waits for them, and re-layouts: none -> 1.19 us  [shards(): fit[0, 0] <= NEAR]
where the time goes in v2:
time: 92.1 us; the launch traced here: 91.9 us
  Pallas kernels  89.8 us (98%)
  local copies, waits for them, and re-layouts  1.2 us (1%)
    pallas_call x1, Pallas kernels, route(): pl.pallas_call(functools.partial(expert_kernel, quick), out_shape=(jax.Sh...  84.3 us
    pallas_call x1, Pallas kernels, mix(): pl.pallas_call(mix_kernel, grid=(tok_rows // tile,), out_shape=jax.ShapeD...  5.54 us

profile of v2, /device:TPU:1, one launch (start us, length us, event | category | flops | bytes accessed | tf_op | source)
XLA Modules:
  0.0 91.9 jit_solution(2472302372100590580)
XLA Ops:
  0.0 0.0 copy-start
  0.0 0.0 copy-start.1
  0.0 84.3 %experts.1 = (bf16[512,512]{1,0:T(8,128)(2,1)S(1)}, f32[512,128]{1,0:T(8,128)S(1)}, f32[8,128]{1,0:T(8,128)}) custom-call(s32[8,512]{1,0:T(8,128)} %picks_ref.1, bf16[4096,512]{1,0:T(8,128)(2,1)} %tok_hbm.1, f32[512,256]{1,0:T(8,128)} %wr_hbm.1, bf16[4096,512]{1,0:T(8,128)(2,1)} %bitcast.11, bf16[4096,512]{1,0:T(8,128)(2,1)} %bitcast.13, ...), custom_call_target="tpu_custom_call" | custom-call | flops 11000000512 | bytes 18874368 | tf_op jit(solution)/shard_map/experts/pallas_call | solution.py:553
  84.3 1.2 %slice.3 = f32[1,1]{1,0:T(1,128)} slice(f32[8,128]{1,0:T(8,128)} %get-tuple-element.37), slice={[0:1], [0:1]} | slice | bytes 8 | tf_op jit(solution)/shard_map/slice | solution.py:641
  86.1 0.0 copy-done
  86.1 0.0 copy-done.1
  86.2 5.7 %conditional.1 = (bf16[4096,512]{1,0:T(8,128)(2,1)}) conditional(s32[]{:T(128)} %bitcast.7, (s32[8,512]{1,0:T(8,128)S(1)}, bf16[1,4096,512]{2,1,0:T(8,128)(2,1)}, bf16[1,4096,512]{2,1,0:T(8,128)(2,1)}, bf16[1,512,4096]{2,1,0:T(8,128)(2,1)}, bf16[4096,512]{1,0:T(8,128)(2,1)}, /*index=5*/f32[512,256]{1,0:T(8,128)S(1)}) %tuple.18, ...), branch_computations={%region_0.0_spmd, %region_1.0_spmd} | conditional | flops 28179869696 | bytes 25264136 | solution.py:641
  86.3 5.5 %mix.3 = bf16[4096,512]{1,0:T(8,128)(2,1)} custom-call(f32[512,128]{1,0:T(8,128)S(1)} %get-tuple-element.32.index_ref, bf16[512,512]{1,0:T(8,128)(2,1)S(1)} %get-tuple-element.33.back_ref), custom_call_target="tpu_custom_call" | custom-call | flops 2147483648 | bytes 6291456 | tf_op jit(solution)/shard_map/cond/branch_1_fun/mix/pallas_call | solution.py:612
Async XLA Ops:
  0.0 86.1 %copy-start = (s32[8,512]{1,0:T(8,128)S(1)}, s32[8,512]{1,0:T(8,128)}, u32[]{:S(2)}) copy-start(s32[8,512]{1,0:T(8,128)} %picks_ref.1) | copy-start | bytes 49156
  0.0 86.1 %copy-start.1 = (f32[512,256]{1,0:T(8,128)S(1)}, f32[512,256]{1,0:T(8,128)}, u32[]{:S(2)}) copy-start(f32[512,256]{1,0:T(8,128)} %wr_hbm.1) | copy-start | bytes 1572868

commit v3 on v2

v3 whole, which is shorter than its diff:
```python
import functools

import jax
import jax.numpy as jnp
from jax import lax
from jax.experimental import pallas as pl
from jax.experimental.pallas import tpu as pltpu
from jax.sharding import PartitionSpec as P

MESH = pl.DeviceIdType.MESH
BF16 = jnp.bfloat16
F32 = jnp.float32
DP = 16
GRP = 8
NEAR = 16
BLK = 256
ROWS = 32
HALF = 16


def iota(shape, dim, dtype=jnp.int32):
    out = lax.broadcasted_iota(jnp.int32, shape, dim)
    return out if dtype == jnp.int32 else out.astype(dtype)


def earlier(n):
    return ones(iota((n, n), 0) < iota((n, n), 1))


def ones(mask):
    return jnp.where(mask, 1.0, 0.0).astype(BF16)


def mm(a, b):
    return jnp.dot(a, b, preferred_element_type=F32)


def over(values):
    return jnp.sum(values, axis=0, keepdims=True)


def best(hit, value):
    return jnp.max(jnp.where(hit, value, -1.0), axis=1, keepdims=True)


def fill_onehot(onehot, index):
    rows = index.shape[0]
    high = jnp.floor(index * (1.0 / 128.0))
    lane = iota((rows, 128), 1, F32)
    low = ones(index - high * 128.0 == lane)
    high = high.astype(BF16)
    for t in range(onehot.shape[1] // 128):
        onehot[:, t * 128 : (t + 1) * 128] = jnp.where(high == float(t), low, 0.0).astype(BF16)


def place_picks(picks_ref, me, tok_rows, index_ref, spread, fit_ref):
    flight, cap = picks_ref.shape
    n_pair = flight * DP
    tri = earlier(cap)
    picks = picks_ref[...]
    owner = picks // tok_rows
    local = (picks - owner * tok_rows).astype(F32)
    dev = iota((DP, cap), 0)
    dev_f = dev.astype(F32)
    at_me = dev == me
    owned = [ones(dev == owner[q : q + 1]) for q in range(flight)]
    stacked = jnp.concatenate(owned, axis=0)
    owned = [o.astype(F32) for o in owned]
    before = mm(stacked, tri)
    count = mm(stacked, jnp.full((cap, cap), 1.0, BF16))
    room = jnp.maximum(ROWS - count, 0.0)
    r, c = iota((n_pair, n_pair), 0), iota((n_pair, n_pair), 1)
    turn = 2 * (r // DP) + 1
    in_turn = (c + DP - turn % DP) % DP < (r + DP - turn % DP) % DP
    room_before = mm(ones((r // DP == c // DP) & in_turn), room.astype(BF16))
    earlier_expert = ones((r % DP == c % DP) & (c // DP < r // DP))

    def of(values, q):
        return values[q * DP : (q + 1) * DP]

    rank = [over(owned[q] * of(before, q)) for q in range(flight)]
    extra = [rank[q] >= ROWS for q in range(flight)]
    extra_no = mm(jnp.concatenate([ones(e) for e in extra], axis=0), tri)
    mine = [owner[q : q + 1] == me for q in range(flight)]
    sends, takes, to_me, fits = [], [], [], jnp.zeros((DP, DP), F32)
    for q in range(flight):
        no = extra_no[q : q + 1]
        first = of(room_before, q)
        dest = jnp.where(
            extra[q] & (no >= first) & (no < first + of(room, q)), 1.0, 0.0
        )
        to_me.append(over(jnp.where(at_me, dest, 0.0)))
        sends.append(jnp.where(mine[q], dest, 0.0).astype(BF16))
        takes.append((owned[q] * to_me[q]).astype(BF16))
        fits = fits + lax.dot_general(
            owned[q].astype(BF16), dest.astype(BF16), (((1,), (1,)), ((), ())),
            preferred_element_type=F32,
        )
    fit_ref[0, 0] = jnp.max(fits)

    def keys(hits):
        hits = jnp.concatenate(hits, axis=0)
        counts = mm(hits, jnp.full((cap, cap), 1.0, BF16)).astype(BF16)
        number = mm(hits, tri) + mm(earlier_expert, counts)
        hits = hits.astype(F32)
        return [over(of(hits, q) * (of(number, q) + NEAR * dev_f)) for q in range(flight)]

    n_far = DP * NEAR
    send_key, take_key = keys(sends), keys(takes)
    slot = iota((n_far, cap), 0, F32)
    far = jnp.full((n_far, cap), -1.0, F32)
    for q in range(flight):
        key = jnp.where(mine[q] & extra[q], send_key[q], -1.0)
        far = jnp.where(slot == key, local[q : q + 1], far)
    far = jnp.max(far, axis=1, keepdims=True)
    index_ref[pl.ds(BLK, n_far), :] = jnp.broadcast_to(far, (n_far, 128))
    slot = iota((ROWS, cap), 0, F32)
    column = iota((ROWS, n_far), 1, F32)
    for q in range(flight):
        key = jnp.where(mine[q], rank[q], -1.0)
        own = best(slot == key, local[q : q + 1])
        index_ref[pl.ds(q * ROWS, ROWS), :] = jnp.broadcast_to(own, (ROWS, 128))
        place = extra_no[q : q + 1] + over(
            jnp.where(at_me, of(count, q) - of(room_before, q), 0.0)
        )
        place = jnp.where(to_me[q] > 0.0, place, -1.0)
        source = best(slot == place, take_key[q])
        spread[pl.ds(q * ROWS, ROWS), :] = ones(source == column)


def expert_kernel(
    quick,
    picks_ref, tok_hbm, wr_hbm, wg_hbm, wu_hbm, wd_hbm,
    back_ref, high_ref, low_ref, fit_ref,
    index_ref, tok, wr, wg, wu, wd, onehot, packed, arrived, spread, rows, logit_part, logit_all,
    x, hidden, part, core_in, sum_in, weighted, returned, outgoing,
    load_sem, own_sem,
    tok_ss, tok_rs, row_ss, row_rs, log_ss, log_rs, ag_ss, ag_rs, sib_ss, sib_rs,
    core_ss, core_rs, rs_ss, rs_rs, ret_ss, ret_rs, out_ss, out_rs,
):
    cap = packed.shape[1]
    d, g = lax.axis_index("dp"), lax.axis_index("group")
    y, xl, core = d // 4, (d // 2) % 2, d % 2
    tok_rows = tok.shape[0]
    feats = tok.shape[1]

    def block(yy, xx, cc):
        return (yy * 2 + xx) * 2 + cc

    up, down, far = (y + 1) % 4, (y + 3) % 4, (y + 2) % 4
    ox, oc = 1 - xl, 1 - core
    to_up = (block(up, xl, core), g)
    to_down = (block(down, xl, core), g)
    to_x = (block(y, ox, core), g)
    to_core = (block(y, xl, oc), g)

    sent = []

    def remote(src, dst, ss, rs, device):
        return pltpu.make_async_remote_copy(
            src_ref=src, dst_ref=dst, send_sem=ss, recv_sem=rs, device_id=device, device_id_type=MESH
        )

    def send(src, dst, ss, rs, device):
        copy = remote(src, dst, ss, rs, device)
        copy.start()
        sent.append(copy)
        return copy

    loads = []
    for i, (src, dst) in enumerate(
        ((tok_hbm, tok), (wr_hbm, wr), (wg_hbm, wg), (wu_hbm, wu), (wd_hbm, wd))
    ):
        copy = pltpu.make_async_copy(src, dst, load_sem.at[i])
        if i < 1:
            copy.start()
        loads.append(copy)

    barrier = pltpu.get_barrier_semaphore()
    for k in range(1, DP):
        pl.semaphore_signal(barrier, inc=1, device_id=((d + k) % DP, g), device_id_type=MESH)
    for k in range(1, GRP):
        pl.semaphore_signal(barrier, inc=1, device_id=(d, (g + k) % GRP), device_id_type=MESH)

    if quick:
        place_picks(picks_ref, d, tok_rows, index_ref, spread, fit_ref)
    else:
        tri = earlier(BLK)
        local = picks_ref[...] - d * tok_rows
        mine = (local >= 0) & (local < tok_rows)
        rank = jnp.dot(
            jnp.where(mine, 1.0, 0.0).astype(BF16), tri, preferred_element_type=F32
        )
        rank = jnp.where(mine, rank, -1.0)
        local = local.astype(F32)
        slot_rank = iota((cap, BLK), 0, F32)
        for b in range(DP):
            chosen = jnp.where(slot_rank == rank[b : b + 1, :], local[b : b + 1, :], -1.0)
            index = jnp.max(chosen, axis=1, keepdims=True)
            index_ref[pl.ds(b * cap, cap), :] = jnp.broadcast_to(index, (cap, 128))

        owner = picks_ref[pl.ds(d, 1), :] // tok_rows
        is_owner = jnp.where(iota((DP, BLK), 0) == owner, 1.0, 0.0)
        ranks = jnp.dot(is_owner.astype(BF16), tri, preferred_element_type=F32)
        place = jnp.sum(is_owner * ranks, axis=0, keepdims=True) + owner.astype(F32) * cap
        spread[...] = jnp.where(iota((DP * cap, BLK), 0, F32) == place, 1.0, 0.0).astype(BF16)
        fit_ref[0, 0] = 0.0

    loads[0].wait()
    for copy in loads[1:]:
        copy.start()
    if quick:
        fill_onehot(onehot, index_ref[pl.ds(BLK, DP * cap), :])
        packed[...] = mm(onehot[...], tok[...]).astype(BF16).reshape(DP, cap, feats)
        pl.semaphore_wait(barrier, DP - 1 + GRP - 1)
        for k in range(1, DP):
            to = (d + k) % DP
            send(packed.at[to], arrived.at[d], tok_ss.at[k], tok_rs.at[k], (to, g))
        arrived[d] = jnp.zeros((cap, feats), BF16)
        fill_onehot(onehot, index_ref[pl.ds(0, BLK), :])
        kept = mm(onehot[...], tok[...])
    else:
        pl.semaphore_wait(barrier, DP - 1 + GRP - 1)

        def gather(step, carry):
            first = (d + 1 + step) % DP
            fill_onehot(onehot, index_ref[pl.ds(pl.multiple_of(first * cap, 16), cap), :])
            packed[first] = mm(onehot[...], tok[...]).astype(BF16)
            k = (first - d + DP) % DP

            @pl.when(first != d)
            def _():
                remote(packed.at[first], arrived.at[d], tok_ss.at[k], tok_rs.at[k], (first, g)).start()

            return carry

        lax.fori_loop(0, DP, gather, 0)
        own = pltpu.make_async_copy(packed.at[d], arrived.at[d], own_sem.at[6])
        own.start()
        own.wait()
    loads[1].wait()
    hi = wr[...].astype(BF16)
    lo = (wr[...] - hi.astype(F32)).astype(BF16)
    for k in range(1, DP):
        frm = (d - k + DP) % DP
        remote(packed.at[frm], arrived.at[frm], tok_ss.at[k], tok_rs.at[k], (frm, g)).wait_recv()

    came = arrived[...].reshape(DP * cap, feats)
    if quick:
        taken = (mm(spread[...], came) + kept).astype(BF16)
    else:
        taken = lax.dot_general(
            spread[...], came, (((0,), (0,)), ((), ())), preferred_element_type=F32
        ).astype(BF16)
    rows[...] = taken.reshape(GRP, ROWS, feats)
    mine_cols = pl.ds(pl.multiple_of(g * feats, feats), feats)
    yx = y * 2 + xl

    def half_rows(f):
        return pl.ds(f * HALF, HALF)

    for f in range(2):
        for k in range(1, GRP):
            q = (g + k) % GRP
            send(
                rows.at[q, half_rows(f)], x.at[f, yx, core, :, mine_cols],
                row_ss.at[f, k], row_rs.at[f, k], (d, q),
            )
    own_rows = []
    for f in range(2):
        copy = pltpu.make_async_copy(
            rows.at[g, half_rows(f)], x.at[f, yx, core, :, mine_cols], own_sem.at[f]
        )
        copy.start()
        own_rows.append(copy)
    logits = mm(taken, hi) + mm(taken, lo)
    logit_part[...] = logits.reshape(GRP, ROWS, logits.shape[1])

    wide = x.shape[4]
    units = wg.shape[1]
    n_half = DP * HALF
    quarter = wide // 4
    left, right = pl.ds(0, 2 * quarter), pl.ds(2 * quarter, 2 * quarter)
    right_a, right_b = pl.ds(2 * quarter, quarter), pl.ds(3 * quarter, quarter)
    own_p, x_p = y * 2 + xl, y * 2 + ox
    up_p, down_p, far_p = up * 2 + xl, down * 2 + xl, far * 2 + xl
    up_x, down_x, far_x = up * 2 + ox, down * 2 + ox, far * 2 + ox
    at_place = (own_p, x_p, up_p, up_x, down_p, down_x, far_p, far_x)

    def ag(f, i, p, cols, to):
        ref = x.at[f, p, core, :, cols]
        send(ref, ref, ag_ss.at[f, i], ag_rs.at[f, i], to)

    def got(f, i, p, cols):
        ref = x.at[f, p, core, :, cols]
        remote(ref, ref, ag_ss.at[f, i], ag_rs.at[f, i], to_x).wait_recv()

    def sib(f, p, cols):
        i = [n for n in range(8) if at_place[n] is p][0] * 2 + (cols is right)
        ref = x.at[f, p, core, :, cols]
        send(ref, ref, sib_ss.at[f, i], sib_rs.at[f, i], to_core)

    def sibs(f):
        for i in range(16):
            ref = x.at[f, at_place[i // 2], oc, :, (left, right)[i % 2]]
            remote(ref, ref, sib_ss.at[f, i], sib_rs.at[f, i], to_core).wait_recv()

    def own_out(f):
        own_rows[f].wait()
        for k in range(1, GRP):
            frm = (g - k + GRP) % GRP
            cols = pl.ds(pl.multiple_of(frm * feats, feats), feats)
            remote(
                rows.at[frm, half_rows(f)], x.at[f, yx, core, :, cols],
                row_ss.at[f, k], row_rs.at[f, k], (d, frm),
            ).wait_recv()
        ag(f, 0, own_p, left, to_x)
        ag(f, 7, own_p, right, to_up)
        ag(f, 8, own_p, right, to_down)
        ag(f, 1, own_p, left, to_up)
        ag(f, 2, own_p, left, to_down)
        ag(f, 9, own_p, right, to_x)
        sib(f, own_p, left)
        sib(f, own_p, right)

    def relay_near(f):
        got(f, 0, x_p, left)
        ag(f, 3, x_p, left, to_up)
        ag(f, 4, x_p, left, to_down)
        sib(f, x_p, left)
        got(f, 8, up_p, right)
        ag(f, 11, up_p, right_b, to_down)
        ag(f, 13, up_p, right, to_x)
        sib(f, up_p, right)
        got(f, 7, down_p, right)
        ag(f, 10, down_p, right_a, to_up)
        ag(f, 12, down_p, right, to_x)
        sib(f, down_p, right)

    def relay_left(f):
        got(f, 1, down_p, left)
        ag(f, 5, down_p, left, to_up)
        sib(f, down_p, left)
        got(f, 2, up_p, left)
        sib(f, up_p, left)
        got(f, 9, x_p, right)
        sib(f, x_p, right)

    def relay_far(f):
        got(f, 4, up_x, left)
        ag(f, 6, up_x, left, to_down)
        sib(f, up_x, left)
        got(f, 10, far_p, right_a)
        got(f, 11, far_p, right_b)
        ag(f, 14, far_p, right, to_x)
        sib(f, far_p, right)

    def last_near(f):
        got(f, 3, down_x, left)
        sib(f, down_x, left)
        got(f, 13, up_x, right)
        sib(f, up_x, right)
        got(f, 12, down_x, right)
        sib(f, down_x, right)

    def last_far(f):
        got(f, 5, far_p, left)
        sib(f, far_p, left)
        got(f, 6, far_x, left)
        sib(f, far_x, left)
        got(f, 14, far_x, right)
        sib(f, far_x, right)

    def into_hidden(f, step):
        cols = pl.ds(step * (units // 2), units // 2)
        xs = x[f].reshape(n_half, wide)
        gate = mm(xs, wg[:, cols])
        lift = mm(xs, wu[:, cols])
        hidden[f, :, cols] = (gate / (1.0 + jnp.exp(-gate)) * lift).astype(BF16)

    def out_of_hidden(f, side):
        hs = hidden[f]

        def tile(step, carry):
            cols = pl.ds(pl.multiple_of(side * 2 * quarter + step * 512, 512), 512)
            part[f, :, :, :, cols] = mm(hs, wd[:, cols]).astype(BF16).reshape(DP // 2, 2, HALF, 512)
            return carry

        lax.fori_loop(0, 2 * quarter // 512, tile, 0)
        cols = (left, right)[side]
        send(
            part.at[f, :, oc, :, cols], core_in.at[f, :, :, cols],
            core_ss.at[f, side], core_rs.at[f, side], to_core,
        )

    def add_sibling(f, side):
        cols = (left, right)[side]
        ref = core_in.at[f, :, :, cols]
        remote(ref, ref, core_ss.at[f, side], core_rs.at[f, side], to_core).wait_recv()
        for p in (far_p, far_x, up_p, up_x, down_p, down_x, own_p, x_p):
            part[f, p, core, :, cols] = (
                part[f, p, core, :, cols].astype(F32) + core_in[f, p, :, cols].astype(F32)
            ).astype(BF16)

    def rs(f, i, p, cols, to):
        send(part.at[f, p, core, :, cols], sum_in.at[f, i, :, cols], rs_ss.at[f, i], rs_rs.at[f, i], to)

    def rs_value(f, i, cols):
        ref = sum_in.at[f, i, :, cols]
        remote(ref, ref, rs_ss.at[f, i], rs_rs.at[f, i], to_x).wait_recv()
        return ref[...].astype(F32)

    def add(f, i, p, cols):
        part[f, p, core, :, cols] = (
            part[f, p, core, :, cols].astype(F32) + rs_value(f, i, cols)
        ).astype(BF16)

    def first_left(f):
        add_sibling(f, 0)
        rs(f, 0, far_p, left, to_up)
        rs(f, 1, far_x, left, to_down)
        rs(f, 2, up_x, left, to_up)
        rs(f, 3, down_p, left, to_down)

    def first_right(f):
        add_sibling(f, 1)
        rs(f, 7, far_x, right, to_x)
        rs(f, 8, up_x, right, to_x)
        rs(f, 9, down_x, right, to_x)
        rs(f, 10, x_p, right, to_x)

    def relay_sums(f):
        add(f, 7, far_p, right)
        rs(f, 13, far_p, right_a, to_up)
        rs(f, 14, far_p, right_b, to_down)
        add(f, 0, up_p, left)
        rs(f, 4, up_p, left, to_up)
        add(f, 1, down_x, left)
        rs(f, 5, down_x, left, to_down)

    def relay_right(f):
        add(f, 8, up_p, right)
        add(f, 13, up_p, right_a)
        rs(f, 11, up_p, right, to_up)
        add(f, 9, down_p, right)
        add(f, 14, down_p, right_b)
        rs(f, 12, down_p, right, to_down)

    def relay_x(f):
        value = part[f, x_p, core, :, left].astype(F32) + rs_value(f, 2, left) + rs_value(f, 5, left)
        part[f, x_p, core, :, left] = value.astype(BF16)
        rs(f, 6, x_p, left, to_x)

    def whole_sums(f):
        value = part[f, own_p, core, :, right].astype(F32) + rs_value(f, 10, right)
        value = (value + rs_value(f, 11, right) + rs_value(f, 12, right)).astype(BF16).astype(F32)
        share = router_share()[f * HALF : (f + 1) * HALF]
        weighted[f, :, right] = (value * share).astype(BF16)
        value = part[f, own_p, core, :, left].astype(F32) + rs_value(f, 3, left) + rs_value(f, 4, left)
        value = (value + rs_value(f, 6, left)).astype(BF16).astype(F32)
        weighted[f, :, left] = (value * share).astype(BF16)
        to_rows = returned.at[pl.ds(pl.multiple_of(g * ROWS + f * HALF, HALF), HALF)]
        for k in range(1, GRP):
            q = (g + k) % GRP
            cols = pl.ds(pl.multiple_of(q * feats, feats), feats)
            send(weighted.at[f, :, cols], to_rows, ret_ss.at[f, k], ret_rs.at[f, k], (d, q))
        copy = pltpu.make_async_copy(weighted.at[f, :, mine_cols], to_rows, own_sem.at[2 + f])
        copy.start()
        own_rows.append(copy)

    share_of = []

    def router_share():
        if not share_of:
            own_logits.wait()
            for k in range(1, GRP):
                frm = (g - k + GRP) % GRP
                remote(logit_part.at[frm], logit_all.at[frm], log_ss.at[k], log_rs.at[k], (d, frm)).wait_recv()
            logits = logit_all[0]
            for q in range(1, GRP):
                logits = logits + logit_all[q]
            grown = jnp.exp(logits - jnp.max(logits, axis=1, keepdims=True))
            column = iota(logits.shape, 1) == g * (logits.shape[1] // GRP)
            picked = jnp.sum(jnp.where(column, grown, 0.0), axis=1, keepdims=True)
            share_of.append(picked / jnp.sum(grown, axis=1, keepdims=True))
        return share_of[0]

    own_out(0)
    relay_near(0)
    own_out(1)
    relay_left(0)
    relay_far(0)
    relay_near(1)
    last_near(0)
    relay_left(1)
    last_far(0)
    sibs(0)
    loads[2].wait()
    loads[3].wait()
    into_hidden(0,0)
    relay_far(1)
    into_hidden(0,1)
    last_near(1)
    loads[4].wait()
    out_of_hidden(0,1)
    out_of_hidden(0,0)
    first_right(0)
    first_left(0)
    last_far(1)
    for k in range(1, GRP):
        q = (g + k) % GRP
        send(logit_part.at[q], logit_all.at[g], log_ss.at[k], log_rs.at[k], (d, q))
    own_logits = pltpu.make_async_copy(logit_part.at[g], logit_all.at[g], own_sem.at[4])
    own_logits.start()
    index = index_ref[...].T
    top = jnp.floor(index * (1.0 / 128.0))
    high_ref[...] = top.astype(BF16)
    low_ref[...] = ones(index - top * 128.0 == iota(index.shape, 0, F32))
    sibs(1)
    into_hidden(1,0)
    relay_sums(0)
    into_hidden(1,1)
    relay_right(0)
    out_of_hidden(1,1)
    relay_x(0)
    out_of_hidden(1,0)
    first_right(1)
    first_left(1)
    whole_sums(0)
    relay_sums(1)
    relay_right(1)
    relay_x(1)
    whole_sums(1)
    own_rows[2].wait()
    own_rows[3].wait()
    for f in range(2):
        for k in range(1, GRP):
            frm = (g - k + GRP) % GRP
            frm_rows = returned.at[pl.ds(pl.multiple_of(frm * ROWS + f * HALF, HALF), HALF)]
            remote(frm_rows, frm_rows, ret_ss.at[f, k], ret_rs.at[f, k], (d, frm)).wait_recv()

    block_rows = returned[...]
    if quick:
        base = BLK
        kept_home = pltpu.make_async_copy(returned, back_ref.at[pl.ds(0, BLK)], own_sem.at[5])
        kept_home.start()
        back = lax.dot_general(
            spread[...], block_rows, (((0,), (0,)), ((), ())), preferred_element_type=F32
        )
    else:
        base = 0
        back = mm(spread[...], block_rows)
    outgoing[...] = back.astype(BF16).reshape(DP, cap, feats)
    to_rows = back_ref.at[pl.ds(pl.multiple_of(base + d * cap, 16), cap)]
    for k in range(1, DP):
        to = (d + k) % DP
        send(outgoing.at[to], to_rows, out_ss.at[k], out_rs.at[k], (to, g))
    own = pltpu.make_async_copy(outgoing.at[d], to_rows, own_sem.at[6])
    own.start()
    own.wait()
    if quick:
        kept_home.wait()
    for k in range(1, DP):
        frm = (d - k + DP) % DP
        frm_rows = back_ref.at[pl.ds(pl.multiple_of(base + frm * cap, 16), cap)]
        remote(outgoing.at[frm], frm_rows, out_ss.at[k], out_rs.at[k], (frm, g)).wait_recv()

    if not quick:
        for k in range(1, DP):
            to = (d + k) % DP
            remote(packed.at[to], arrived.at[d], tok_ss.at[k], tok_rs.at[k], (to, g)).wait_send()
    for copy in sent:
        copy.wait_send()


def mix_kernel(high, low, back, out_hbm, out, sem):
    tile = 512
    n_tile = out.shape[0] // tile
    rows = back.shape[0]

    def copy(t):
        at = pl.ds(pl.multiple_of(t * tile, tile), tile)
        return pltpu.make_async_copy(out.at[at], out_hbm.at[at], sem.at[t])

    def step(t, carry):
        parts = []
        for i in range(tile // 128):
            here = jnp.full((1, rows), jnp.asarray(t * (tile // 128) + i, jnp.int32).astype(F32)).astype(BF16)
            parts.append(jnp.where(high[...] == here, low[...], 0.0))
        at = pl.ds(pl.multiple_of(t * tile, tile), tile)
        out[at, :] = mm(jnp.concatenate(parts, axis=0), back[...]).astype(BF16)
        copy(t).start()
        return carry

    if rows > 1024:
        lax.fori_loop(0, n_tile, step, 0)
    else:
        for t in range(n_tile):
            step(t, 0)
    for t in range(n_tile):
        copy(t).wait()


def route(tokens, router_weight, gate_weight, up_weight, down_weight, picks, quick):
    cap = NEAR if quick else BLK
    packed = DP * cap
    n_back = packed + (BLK if quick else 0)
    tok_rows, feats = tokens.shape
    units, wide = down_weight.shape[1:]
    n_exp = router_weight.shape[1]
    dma = pltpu.SemaphoreType.DMA
    any_spec = pl.BlockSpec(memory_space=pl.ANY)
    vmem_spec = pl.BlockSpec(memory_space=pltpu.VMEM)
    return pl.pallas_call(
        functools.partial(expert_kernel, quick),
        out_shape=(
            jax.ShapeDtypeStruct((n_back, feats), BF16),
            jax.ShapeDtypeStruct((128, n_back), BF16),
            jax.ShapeDtypeStruct((128, n_back), BF16),
            jax.ShapeDtypeStruct((1, 1), F32),
        ),
        in_specs=[vmem_spec] + [any_spec] * 5,
        out_specs=(any_spec, vmem_spec, vmem_spec, pl.BlockSpec(memory_space=pltpu.SMEM)),
        scratch_shapes=[
            pltpu.VMEM((n_back, 128), F32),
            pltpu.VMEM((tok_rows, feats), BF16),
            pltpu.VMEM((feats, n_exp), F32),
            pltpu.VMEM((wide, units), BF16),
            pltpu.VMEM((wide, units), BF16),
            pltpu.VMEM((units, wide), BF16),
            pltpu.VMEM((BLK, tok_rows), BF16),
            pltpu.VMEM((DP, cap, feats), BF16),
            pltpu.VMEM((DP, cap, feats), BF16),
            pltpu.VMEM((BLK, packed) if quick else (packed, BLK), BF16),
            pltpu.VMEM((GRP, ROWS, feats), BF16),
            pltpu.VMEM((GRP, ROWS, n_exp), F32),
            pltpu.VMEM((GRP, ROWS, n_exp), F32),
            pltpu.VMEM((2, DP // 2, 2, HALF, wide), BF16),
            pltpu.VMEM((2, DP * HALF, units), BF16),
            pltpu.VMEM((2, DP // 2, 2, HALF, wide), BF16),
            pltpu.VMEM((2, DP // 2, HALF, wide), BF16),
            pltpu.VMEM((2, 15, HALF, wide), BF16),
            pltpu.VMEM((2, HALF, wide), BF16),
            pltpu.VMEM((BLK, feats), BF16),
            pltpu.VMEM((DP, cap, feats), BF16),
            dma((5,)),
            dma((7,)),
            dma((DP,)), dma((DP,)),
            dma((2, GRP)), dma((2, GRP)),
            dma((GRP,)), dma((GRP,)),
            dma((2, 15)), dma((2, 15)),
            dma((2, 16)), dma((2, 16)),
            dma((2, 2)), dma((2, 2)),
            dma((2, 15)), dma((2, 15)),
            dma((2, GRP)), dma((2, GRP)),
            dma((DP,)), dma((DP,)),
        ],
        compiler_params=pltpu.CompilerParams(
            collective_id=1 if quick else 2, has_side_effects=True, vmem_limit_bytes=60 * 2**20
        ),
        cost_estimate=pl.CostEstimate(
            flops=11 * 10**9, bytes_accessed=18 * 2**20, transcendentals=512 * 512
        ),
        name="experts" if quick else "experts_any",
    )(
        picks, tokens, router_weight, gate_weight[0], up_weight[0], down_weight[0]
    )


def mix(back, high, low, tok_rows):
    rows, feats = back.shape
    vmem_spec = pl.BlockSpec(memory_space=pltpu.VMEM)
    return pl.pallas_call(
        mix_kernel,
        out_shape=jax.ShapeDtypeStruct((tok_rows, feats), BF16),
        in_specs=[vmem_spec] * 3,
        out_specs=pl.BlockSpec(memory_space=pl.ANY),
        scratch_shapes=[pltpu.VMEM((tok_rows, feats), BF16), pltpu.SemaphoreType.DMA((tok_rows // 512,))],
        compiler_params=pltpu.CompilerParams(vmem_limit_bytes=60 * 2**20),
        cost_estimate=pl.CostEstimate(
            flops=2 * tok_rows * rows * feats, bytes_accessed=6 * 2**20, transcendentals=0
        ),
        name="mix",
    )(high, low, back)


def shards(tokens, router_weight, gate_weight, up_weight, down_weight, picks):
    tok_rows = tokens.shape[0]
    flight, capacity = picks.shape
    args = (tokens, router_weight, gate_weight, up_weight, down_weight)
    back, high, low, fit = route(*args, picks, True)

    def any_picks():
        blocks = picks.reshape(flight, DP, ROWS).transpose(1, 0, 2).reshape(DP, BLK)
        back, high, low, _ = route(*args, blocks, False)
        return mix(back, high, low, tok_rows)

    return lax.cond(fit[0, 0] <= NEAR, lambda: mix(back, high, low, tok_rows), any_picks)


def solution(mesh):
    in_specs = (
        P("dp", "group"),
        P("group", None),
        P("group", None, "dp"),
        P("group", None, "dp"),
        P("group", "dp", None),
        P(),
    )
    out_specs = P("dp", "group")
    return jax.shard_map(shards, mesh=mesh, in_specs=in_specs, out_specs=out_specs, check_vma=False)
```

time: 92.1 us -> 81 us (0.88)
  Pallas kernels: 89.8 us -> 79.7 us
  local copies, waits for them, and re-layouts: 1.2 us -> 0.01 us
    pallas_call x1, Pallas kernels: 84.3 us -> 76.5 us  [route(): pl.pallas_call(functools.partial(expert_kernel, quick), out_shape=(jax.Sh...]
    pallas_call x1, Pallas kernels: 5.54 us -> 3.21 us  [mix(): pl.pallas_call(mix_kernel, out_shape=jax.ShapeDtypeStruct((tok_rows, feat...]
    slice x1 -> x0, local copies, waits for them, and re-layouts: 1.19 us -> none  [shards(): fit[0, 0] <= NEAR]
where the time goes in v3:
time: 81 us; the launch traced here: 80.8 us
  Pallas kernels  79.7 us (98%)
  between operations  0.9 us (1%)
    pallas_call x1, Pallas kernels, route(): pl.pallas_call(functools.partial(expert_kernel, quick), out_shape=(jax.Sh...  76.5 us
    pallas_call x1, Pallas kernels, mix(): pl.pallas_call(mix_kernel, out_shape=jax.ShapeDtypeStruct((tok_rows, feat...  3.21 us

profile of v3, /device:TPU:1, one launch (start us, length us, event | category | flops | bytes accessed | tf_op | source)
XLA Modules:
  0.0 80.8 jit_solution(12263217326195308250)
XLA Ops:
  0.0 0.0 copy-start
  0.0 0.0 copy-start.1
  0.0 76.5 %experts.1 = (bf16[512,512]{1,0:T(8,128)(2,1)S(1)}, bf16[128,512]{1,0:T(8,128)(2,1)S(1)}, bf16[128,512]{1,0:T(8,128)(2,1)S(1)}, f32[1,1]{1,0:T(1,128)}) custom-call(s32[8,512]{1,0:T(8,128)} %picks_ref.1, bf16[4096,512]{1,0:T(8,128)(2,1)} %tok_hbm.1, f32[512,256]{1,0:T(8,128)} %wr_hbm.1, bf16[4096,512]{1,0:T(8,128)(2,1)} %bitcast.11, ...), custom_call_target="tpu_custom_call" | custom-call | flops 11000000512 | bytes 18874368 | tf_op jit(solution)/shard_map/experts/pallas_call | solution.py:614
  77.2 0.0 copy-done
  77.2 0.0 copy-done.1
  77.2 3.5 %conditional.1 = (bf16[4096,512]{1,0:T(8,128)(2,1)}) conditional(s32[]{:T(128)} %bitcast.7, (s32[8,512]{1,0:T(8,128)S(1)}, bf16[1,4096,512]{2,1,0:T(8,128)(2,1)}, bf16[1,4096,512]{2,1,0:T(8,128)(2,1)}, bf16[1,512,4096]{2,1,0:T(8,128)(2,1)}, bf16[4096,512]{1,0:T(8,128)(2,1)}, /*index=5*/f32[512,256]{1,0:T(8,128)S(1)}) %tuple.18, ...), branch_computations={%region_0.0_spmd, %region_1.0_spmd} | conditional | flops 28179869696 | bytes 25264136 | solution.py:698
  77.5 3.2 %mix.3 = bf16[4096,512]{1,0:T(8,128)(2,1)} custom-call(bf16[128,512]{1,0:T(8,128)(2,1)S(1)} %get-tuple-element.35.high, bf16[128,512]{1,0:T(8,128)(2,1)S(1)} %get-tuple-element.36.low, bf16[512,512]{1,0:T(8,128)(2,1)S(1)} %get-tuple-element.37.back), custom_call_target="tpu_custom_call" | custom-call | flops 2147483648 | bytes 6291456 | tf_op jit(solution)/shard_map/cond/branch_1_fun/mix/pallas_call | solution.py:673
Async XLA Ops:
  0.0 77.2 %copy-start = (s32[8,512]{1,0:T(8,128)S(1)}, s32[8,512]{1,0:T(8,128)}, u32[]{:S(2)}) copy-start(s32[8,512]{1,0:T(8,128)} %picks_ref.1) | copy-start | bytes 49156
  0.0 77.2 %copy-start.1 = (f32[512,256]{1,0:T(8,128)S(1)}, f32[512,256]{1,0:T(8,128)}, u32[]{:S(2)}) copy-start(f32[512,256]{1,0:T(8,128)} %wr_hbm.1) | copy-start | bytes 1572868

commit v4 on v3

--- a/solution.py
+++ b/solution.py
@@ -154,6 +154,23 @@
     to_x = (block(y, ox, core), g)
     to_core = (block(y, xl, oc), g)
 
+    z, xh = g // 2, g % 2
+    dp_moves, grp_moves = [], []
+    for dy, dx, dc in sorted(
+        ((dy, dx, dc) for dy in range(4) for dx in range(2) for dc in range(2)),
+        key=lambda m: -(min(m[0], 4 - m[0]) + m[1]),
+    ):
+        if (dy, dx, dc) != (0, 0, 0):
+            across = (xl + dx) % 2, (core + dc) % 2
+            to, frm = block((y + dy) % 4, *across), block((y + 4 - dy) % 4, *across)
+            dp_moves.append((len(dp_moves) + 1, to, frm))
+    for dz, dx in sorted(
+        ((dz, dx) for dz in range(4) for dx in range(2)), key=lambda m: -(min(m[0], 4 - m[0]) + 2 * m[1])
+    ):
+        if (dz, dx) != (0, 0):
+            to, frm = (z + dz) % 4 * 2 + (xh + dx) % 2, (z + 4 - dz) % 4 * 2 + (xh + dx) % 2
+            grp_moves.append((len(grp_moves) + 1, to, frm))
+
     sent = []
 
     def remote(src, dst, ss, rs, device):
@@ -177,10 +194,10 @@
         loads.append(copy)
 
     barrier = pltpu.get_barrier_semaphore()
-    for k in range(1, DP):
-        pl.semaphore_signal(barrier, inc=1, device_id=((d + k) % DP, g), device_id_type=MESH)
-    for k in range(1, GRP):
-        pl.semaphore_signal(barrier, inc=1, device_id=(d, (g + k) % GRP), device_id_type=MESH)
+    for _, to, _ in dp_moves:
+        pl.semaphore_signal(barrier, inc=1, device_id=(to, g), device_id_type=MESH)
+    for _, to, _ in grp_moves:
+        pl.semaphore_signal(barrier, inc=1, device_id=(d, to), device_id_type=MESH)
 
     if quick:
         place_picks(picks_ref, d, tok_rows, index_ref, spread, fit_ref)
@@ -213,8 +230,7 @@
         fill_onehot(onehot, index_ref[pl.ds(BLK, DP * cap), :])
         packed[...] = mm(onehot[...], tok[...]).astype(BF16).reshape(DP, cap, feats)
         pl.semaphore_wait(barrier, DP - 1 + GRP - 1)
-        for k in range(1, DP):
-            to = (d + k) % DP
+        for k, to, _ in dp_moves:
             send(packed.at[to], arrived.at[d], tok_ss.at[k], tok_rs.at[k], (to, g))
         arrived[d] = jnp.zeros((cap, feats), BF16)
         fill_onehot(onehot, index_ref[pl.ds(0, BLK), :])
@@ -241,8 +257,7 @@
     loads[1].wait()
     hi = wr[...].astype(BF16)
     lo = (wr[...] - hi.astype(F32)).astype(BF16)
-    for k in range(1, DP):
-        frm = (d - k + DP) % DP
+    for k, frm in [(k, frm) for k, _, frm in dp_moves] if quick else [(k, (d - k + DP) % DP) for k in range(1, DP)]:
         remote(packed.at[frm], arrived.at[frm], tok_ss.at[k], tok_rs.at[k], (frm, g)).wait_recv()
 
     came = arrived[...].reshape(DP * cap, feats)
@@ -260,8 +275,7 @@
         return pl.ds(f * HALF, HALF)
 
     for f in range(2):
-        for k in range(1, GRP):
-            q = (g + k) % GRP
+        for k, q, _ in grp_moves:
             send(
                 rows.at[q, half_rows(f)], x.at[f, yx, core, :, mine_cols],
                 row_ss.at[f, k], row_rs.at[f, k], (d, q),
@@ -307,8 +321,7 @@
 
     def own_out(f):
         own_rows[f].wait()
-        for k in range(1, GRP):
-            frm = (g - k + GRP) % GRP
+        for k, _, frm in grp_moves:
             cols = pl.ds(pl.multiple_of(frm * feats, feats), feats)
             remote(
                 rows.at[frm, half_rows(f)], x.at[f, yx, core, :, cols],
@@ -460,8 +473,7 @@
         value = (value + rs_value(f, 6, left)).astype(BF16).astype(F32)
         weighted[f, :, left] = (value * share).astype(BF16)
         to_rows = returned.at[pl.ds(pl.multiple_of(g * ROWS + f * HALF, HALF), HALF)]
-        for k in range(1, GRP):
-            q = (g + k) % GRP
+        for k, q, _ in grp_moves:
             cols = pl.ds(pl.multiple_of(q * feats, feats), feats)
             send(weighted.at[f, :, cols], to_rows, ret_ss.at[f, k], ret_rs.at[f, k], (d, q))
         copy = pltpu.make_async_copy(weighted.at[f, :, mine_cols], to_rows, own_sem.at[2 + f])
@@ -473,8 +485,7 @@
     def router_share():
         if not share_of:
             own_logits.wait()
-            for k in range(1, GRP):
-                frm = (g - k + GRP) % GRP
+            for k, _, frm in grp_moves:
                 remote(logit_part.at[frm], logit_all.at[frm], log_ss.at[k], log_rs.at[k], (d, frm)).wait_recv()
             logits = logit_all[0]
             for q in range(1, GRP):
@@ -507,8 +518,7 @@
     first_right(0)
     first_left(0)
     last_far(1)
-    for k in range(1, GRP):
-        q = (g + k) % GRP
+    for k, q, _ in grp_moves:
         send(logit_part.at[q], logit_all.at[g], log_ss.at[k], log_rs.at[k], (d, q))
     own_logits = pltpu.make_async_copy(logit_part.at[g], logit_all.at[g], own_sem.at[4])
     own_logits.start()
@@ -534,8 +544,7 @@
     own_rows[2].wait()
     own_rows[3].wait()
     for f in range(2):
-        for k in range(1, GRP):
-            frm = (g - k + GRP) % GRP
+        for k, _, frm in grp_moves:
             frm_rows = returned.at[pl.ds(pl.multiple_of(frm * ROWS + f * HALF, HALF), HALF)]
             remote(frm_rows, frm_rows, ret_ss.at[f, k], ret_rs.at[f, k], (d, frm)).wait_recv()
 
@@ -552,16 +561,14 @@
         back = mm(spread[...], block_rows)
     outgoing[...] = back.astype(BF16).reshape(DP, cap, feats)
     to_rows = back_ref.at[pl.ds(pl.multiple_of(base + d * cap, 16), cap)]
-    for k in range(1, DP):
-        to = (d + k) % DP
+    for k, to, _ in dp_moves:
         send(outgoing.at[to], to_rows, out_ss.at[k], out_rs.at[k], (to, g))
     own = pltpu.make_async_copy(outgoing.at[d], to_rows, own_sem.at[6])
     own.start()
     own.wait()
     if quick:
         kept_home.wait()
-    for k in range(1, DP):
-        frm = (d - k + DP) % DP
+    for k, _, frm in dp_moves:
         frm_rows = back_ref.at[pl.ds(pl.multiple_of(base + frm * cap, 16), cap)]
         remote(outgoing.at[frm], frm_rows, out_ss.at[k], out_rs.at[k], (frm, g)).wait_recv()
 

time: 81 us -> 80.3 us (level)
  no operation moved by 1% of the time
where the time goes in v4:
time: 80.3 us; the launch traced here: 80.1 us
  Pallas kernels  79 us (98%)
  between operations  0.9 us (1%)
    pallas_call x1, Pallas kernels, route(): pl.pallas_call(functools.partial(expert_kernel, quick), out_shape=(jax.Sh...  75.8 us
    pallas_call x1, Pallas kernels, mix(): pl.pallas_call(mix_kernel, out_shape=jax.ShapeDtypeStruct((tok_rows, feat...  3.21 us

profile of v4, /device:TPU:1, one launch (start us, length us, event | category | flops | bytes accessed | tf_op | source)
XLA Modules:
  0.0 80.1 jit_solution(207807983000686928)
XLA Ops:
  0.0 0.0 copy-start
  0.0 0.0 copy-start.1
  0.0 75.8 %experts.1 = (bf16[512,512]{1,0:T(8,128)(2,1)S(1)}, bf16[128,512]{1,0:T(8,128)(2,1)S(1)}, bf16[128,512]{1,0:T(8,128)(2,1)S(1)}, f32[1,1]{1,0:T(1,128)}) custom-call(s32[8,512]{1,0:T(8,128)} %picks_ref.1, bf16[4096,512]{1,0:T(8,128)(2,1)} %tok_hbm.1, f32[512,256]{1,0:T(8,128)} %wr_hbm.1, bf16[4096,512]{1,0:T(8,128)(2,1)} %bitcast.11, ...), custom_call_target="tpu_custom_call" | custom-call | flops 11000000512 | bytes 18874368 | tf_op jit(solution)/shard_map/experts/pallas_call | solution.py:621
  76.5 0.0 copy-done
  76.5 0.0 copy-done.1
  76.5 3.5 %conditional.1 = (bf16[4096,512]{1,0:T(8,128)(2,1)}) conditional(s32[]{:T(128)} %bitcast.7, (s32[8,512]{1,0:T(8,128)S(1)}, bf16[1,4096,512]{2,1,0:T(8,128)(2,1)}, bf16[1,4096,512]{2,1,0:T(8,128)(2,1)}, bf16[1,512,4096]{2,1,0:T(8,128)(2,1)}, bf16[4096,512]{1,0:T(8,128)(2,1)}, /*index=5*/f32[512,256]{1,0:T(8,128)S(1)}) %tuple.18, ...), branch_computations={%region_0.0_spmd, %region_1.0_spmd} | conditional | flops 28179869696 | bytes 25264136 | solution.py:705
  76.7 3.2 %mix.3 = bf16[4096,512]{1,0:T(8,128)(2,1)} custom-call(bf16[128,512]{1,0:T(8,128)(2,1)S(1)} %get-tuple-element.35.high, bf16[128,512]{1,0:T(8,128)(2,1)S(1)} %get-tuple-element.36.low, bf16[512,512]{1,0:T(8,128)(2,1)S(1)} %get-tuple-element.37.back), custom_call_target="tpu_custom_call" | custom-call | flops 2147483648 | bytes 6291456 | tf_op jit(solution)/shard_map/cond/branch_1_fun/mix/pallas_call | solution.py:680
Async XLA Ops:
  0.0 76.5 %copy-start = (s32[8,512]{1,0:T(8,128)S(1)}, s32[8,512]{1,0:T(8,128)}, u32[]{:S(2)}) copy-start(s32[8,512]{1,0:T(8,128)} %picks_ref.1) | copy-start | bytes 49156
  0.0 76.5 %copy-start.1 = (f32[512,256]{1,0:T(8,128)S(1)}, f32[512,256]{1,0:T(8,128)}, u32[]{:S(2)}) copy-start(f32[512,256]{1,0:T(8,128)} %wr_hbm.1) | copy-start | bytes 1572868

commit v5 on v4

--- a/solution.py
+++ b/solution.py
@@ -223,11 +223,12 @@
         spread[...] = jnp.where(iota((DP * cap, BLK), 0, F32) == place, 1.0, 0.0).astype(BF16)
         fit_ref[0, 0] = 0.0
 
+    if quick:
+        fill_onehot(onehot, index_ref[pl.ds(BLK, DP * cap), :])
     loads[0].wait()
     for copy in loads[1:]:
         copy.start()
     if quick:
-        fill_onehot(onehot, index_ref[pl.ds(BLK, DP * cap), :])
         packed[...] = mm(onehot[...], tok[...]).astype(BF16).reshape(DP, cap, feats)
         pl.semaphore_wait(barrier, DP - 1 + GRP - 1)
         for k, to, _ in dp_moves:

time: 80.3 us -> 80 us (level)
  no operation moved by 1% of the time
where the time goes in v5:
time: 80 us; the launch traced here: 79.8 us
  Pallas kernels  78.9 us (99%)
  between operations  0.88 us (1%)
    pallas_call x1, Pallas kernels, route(): pl.pallas_call(functools.partial(expert_kernel, quick), out_shape=(jax.Sh...  75.7 us
    pallas_call x1, Pallas kernels, mix(): pl.pallas_call(mix_kernel, out_shape=jax.ShapeDtypeStruct((tok_rows, feat...  3.21 us

profile of v5, /device:TPU:1, one launch (start us, length us, event | category | flops | bytes accessed | tf_op | source)
XLA Modules:
  0.0 79.8 jit_solution(14812921668488503449)
XLA Ops:
  0.0 0.0 copy-start
  0.0 0.0 copy-start.1
  0.0 75.7 %experts.1 = (bf16[512,512]{1,0:T(8,128)(2,1)S(1)}, bf16[128,512]{1,0:T(8,128)(2,1)S(1)}, bf16[128,512]{1,0:T(8,128)(2,1)S(1)}, f32[1,1]{1,0:T(1,128)}) custom-call(s32[8,512]{1,0:T(8,128)} %picks_ref.1, bf16[4096,512]{1,0:T(8,128)(2,1)} %tok_hbm.1, f32[512,256]{1,0:T(8,128)} %wr_hbm.1, bf16[4096,512]{1,0:T(8,128)(2,1)} %bitcast.11, ...), custom_call_target="tpu_custom_call" | custom-call | flops 11000000512 | bytes 18874368 | tf_op jit(solution)/shard_map/experts/pallas_call | solution.py:622
  76.4 0.0 copy-done
  76.4 0.0 copy-done.1
  76.4 3.2 %conditional.1 = (bf16[4096,512]{1,0:T(8,128)(2,1)}) conditional(s32[]{:T(128)} %bitcast.7, (s32[8,512]{1,0:T(8,128)S(1)}, bf16[1,4096,512]{2,1,0:T(8,128)(2,1)}, bf16[1,4096,512]{2,1,0:T(8,128)(2,1)}, bf16[1,512,4096]{2,1,0:T(8,128)(2,1)}, bf16[4096,512]{1,0:T(8,128)(2,1)}, /*index=5*/f32[512,256]{1,0:T(8,128)S(1)}) %tuple.18, ...), branch_computations={%region_0.0_spmd, %region_1.0_spmd} | conditional | flops 28179869696 | bytes 25264136 | solution.py:706
  76.4 3.2 %mix.3 = bf16[4096,512]{1,0:T(8,128)(2,1)} custom-call(bf16[128,512]{1,0:T(8,128)(2,1)S(1)} %get-tuple-element.35.high, bf16[128,512]{1,0:T(8,128)(2,1)S(1)} %get-tuple-element.36.low, bf16[512,512]{1,0:T(8,128)(2,1)S(1)} %get-tuple-element.37.back), custom_call_target="tpu_custom_call" | custom-call | flops 2147483648 | bytes 6291456 | tf_op jit(solution)/shard_map/cond/branch_1_fun/mix/pallas_call | solution.py:681
Async XLA Ops:
  0.0 76.4 %copy-start = (s32[8,512]{1,0:T(8,128)S(1)}, s32[8,512]{1,0:T(8,128)}, u32[]{:S(2)}) copy-start(s32[8,512]{1,0:T(8,128)} %picks_ref.1) | copy-start | bytes 49156
  0.0 76.4 %copy-start.1 = (f32[512,256]{1,0:T(8,128)S(1)}, f32[512,256]{1,0:T(8,128)}, u32[]{:S(2)}) copy-start(f32[512,256]{1,0:T(8,128)} %wr_hbm.1) | copy-start | bytes 1572868
